TPU v7x, 32 devices: a whole 2x2x4 slice. The times are simulated.
32 devices in a mesh: pipe: 8 (over z, core), tensor: 4 (over y, x).
Axes of the slice: x: 2, y: 2, z: 4, core: 2. Of those that a mesh axis runs over, the one named last changes fastest.
Arguments:
- section_inputs: bfloat16 [8, 8, 128, 12288], P('pipe', None, None, 'tensor'), may hold values from -6 to 6
- out_grad: bfloat16 [8, 128, 12288], P(None, None, 'tensor'), may hold values from -6 to 6
- w_first: bfloat16 [8, 1, 96, 128, 128], P('pipe', None, 'tensor'), may hold values from -0.5 to 0.5
- w_second: bfloat16 [8, 1, 96, 128, 128], P('pipe', None, 'tensor'), may hold values from -0.5 to 0.5
- drop_flags: int32 [8, 1], P('pipe'), may hold values 0 or 1
- perm: int32 [8, 1, 12288], P('pipe'), may hold values from 0 to 12287, as said below
Outputs:
- input_grads: bfloat16 [8, 8, 128, 12288], P('pipe', None, None, 'tensor')
- grad_first: float32 [8, 1, 96, 128, 128], P('pipe', None, 'tensor')
- grad_second: float32 [8, 1, 96, 128, 128], P('pipe', None, 'tensor')
Inputs may be any that keep to these rules, and one draw needn't show every extreme that they name: For each section and layer, perm is a permutation of 0 to 12287, and for every two block groups g and h exactly 768 of the positions h * 3072 to (h + 1) * 3072 - 1 hold a feature of group g, that is a number from g * 3072 to (g + 1) * 3072 - 1.
All inputs are finite; a program needn't handle non-finite values. No bound on the sum of `drop_flags` on one device may be relied on, other than what follows from the above.
Results may differ from a plain program's by a relative error of at most 0.023.
Values may be sent and summed in bfloat16 or wider, within the bound.
A program may use at most 128 MiB of HBM per device.

v0:
```python
import jax
import jax.numpy as jnp
from jax import lax
from jax.sharding import PartitionSpec as P

gelu_scale = 0.7978845608028654
gelu_cubic = 0.044715


def passed_along(block, axis, distance):
    devices = range(lax.axis_size(axis))
    route = [(i - distance, i) for i in devices if i - distance in devices]
    return lax.ppermute(block, axis, route)


def gelu_value(values):
    inner = gelu_scale * (values + gelu_cubic * values * values * values)
    return 0.5 * values * (1.0 + jnp.tanh(inner))


def gelu_slope(values):
    tangent = jnp.tanh(gelu_scale * (values + gelu_cubic * values * values * values))
    return 0.5 * (1.0 + tangent) + 0.5 * values * (1.0 - tangent * tangent) * gelu_scale * (
        1.0 + 3.0 * gelu_cubic * values * values
    )


def block_forward(values, weight):
    count = weight.shape[0]
    result = jnp.einsum(
        "tbi,bij->tbj",
        values.reshape(values.shape[0], count, -1),
        weight,
        preferred_element_type=jnp.float32,
    )
    return result.reshape(values.shape[0], -1)


def block_backward(values, weight):
    count = weight.shape[0]
    result = jnp.einsum(
        "tbj,bij->tbi",
        values.reshape(values.shape[0], count, -1),
        weight,
        preferred_element_type=jnp.float32,
    )
    return result.reshape(values.shape[0], -1)


def block_outer(left, right, count):
    left_blocks = left.reshape(left.shape[0], count, -1)
    right_blocks = right.reshape(right.shape[0], count, -1)
    return jnp.einsum("tbi,tbj->bij", left_blocks, right_blocks, preferred_element_type=jnp.float32)


def route_tables(source_row, group_index, group_count):
    feat_count = source_row.shape[0] // group_count
    per_peer = feat_count // group_count
    target_rows = source_row.reshape(group_count, feat_count)
    source_group = target_rows // feat_count
    position = jnp.arange(feat_count, dtype=jnp.int32)
    ranking = jnp.where(
        source_group == group_index, position[None, :], feat_count + position[None, :]
    )
    chosen = jnp.argsort(ranking, axis=1)[:, :per_peer]
    send_index = (
        jnp.take_along_axis(target_rows, chosen, axis=1) - group_index * feat_count
    ).reshape(-1)
    own_row = lax.dynamic_slice_in_dim(target_rows, group_index, 1, 0)[0]
    arrival = jnp.argsort(own_row // feat_count * feat_count + position)
    placing = jnp.argsort(arrival)
    gathering = jnp.argsort(send_index)
    return (send_index, arrival, placing, gathering)


def on_device(section_inputs, out_grad, w_first, w_second, drop_flags, perm):
    section_count = lax.axis_size("pipe")
    section_index = lax.axis_index("pipe")
    group_count = lax.axis_size("tensor")
    group_index = lax.axis_index("tensor")
    micro_count = section_inputs.shape[1]
    local_inputs = section_inputs[0]
    first_weights = w_first[0]
    second_weights = w_second[0]
    tables = [route_tables(perm[0, 0], group_index, group_count)]

    def mix_forward(hidden, layer_index):
        send_index, arrival, placing, gathering = tables[layer_index]
        outgoing = jnp.take(hidden, send_index, axis=1)
        mixed = jnp.take(
            lax.all_to_all(outgoing, "tensor", split_axis=1, concat_axis=1, tiled=True),
            placing,
            axis=1,
        )
        branch = block_forward(mixed, second_weights[layer_index])
        return (mixed, branch)

    def mix_backward(grad_mixed, layer_index):
        send_index, arrival, placing, gathering = tables[layer_index]
        returned = lax.all_to_all(
            jnp.take(grad_mixed, arrival, axis=1), "tensor", split_axis=1, concat_axis=1, tiled=True
        )
        return jnp.take(returned, gathering, axis=1)

    block_count = first_weights.shape[1]

    def layer_forward(current, layer_index):
        keep_factor = drop_flags[0, layer_index].astype(jnp.float32)
        before = block_forward(current, first_weights[layer_index])
        hidden = gelu_value(before).astype(jnp.bfloat16)
        mixed, branch = mix_forward(hidden, layer_index)
        following = (current.astype(jnp.float32) + keep_factor * branch).astype(jnp.bfloat16)
        return (following, before, mixed)

    def layer_backward(grad_now, current, before, mixed, layer_index):
        keep_factor = drop_flags[0, layer_index].astype(jnp.float32)
        grad_branch = (keep_factor * grad_now.astype(jnp.float32)).astype(jnp.bfloat16)
        second_part = block_outer(mixed, grad_branch, block_count)
        grad_mixed = block_backward(grad_branch, second_weights[layer_index]).astype(jnp.bfloat16)
        grad_hidden = mix_backward(grad_mixed, layer_index)
        grad_before = (grad_hidden.astype(jnp.float32) * gelu_slope(before)).astype(jnp.bfloat16)
        first_part = block_outer(current, grad_before, block_count)
        back_term = block_backward(grad_before, first_weights[layer_index])
        grad_prior = (grad_now.astype(jnp.float32) + back_term).astype(jnp.bfloat16)
        return (grad_prior, first_part, second_part)

    def run_section(first_input, cotangent):
        layer_inputs = [first_input]
        layer_index = 0
        current = layer_inputs[-1]
        following, before, mixed = layer_forward(current, layer_index)
        layer_inputs.append(following)
        saved_pairs = [(before, mixed)]
        grad_now = cotangent
        layer_index = 0
        current = layer_inputs[layer_index]
        before, mixed = saved_pairs[layer_index]
        grad_now, first_part, second_part = layer_backward(
            grad_now, current, before, mixed, layer_index
        )
        first_list = [first_part]
        second_list = [second_part]
        return (grad_now, jnp.stack(first_list[::-1]), jnp.stack(second_list[::-1]))

    def advance(step_index, carry):
        outgoing, buffer, sum_first, sum_second = carry
        incoming = passed_along(outgoing, "pipe", -1)
        micro_index = step_index - (section_count - 1 - section_index)
        live = (micro_index >= 0) & (micro_index < micro_count)
        clipped = jnp.clip(micro_index, 0, micro_count - 1)
        first_input = lax.dynamic_index_in_dim(local_inputs, clipped, 0, keepdims=False)
        last_grad = lax.dynamic_index_in_dim(out_grad, clipped, 0, keepdims=False)
        cotangent = jnp.where(section_index == section_count - 1, last_grad, incoming)
        grad_in, first_parts, second_parts = run_section(first_input, cotangent)
        previous = lax.dynamic_index_in_dim(buffer, clipped, 0, keepdims=False)
        buffer = lax.dynamic_update_index_in_dim(
            buffer, jnp.where(live, grad_in, previous), clipped, 0
        )
        sum_first = sum_first + jnp.where(live, first_parts, 0.0)
        sum_second = sum_second + jnp.where(live, second_parts, 0.0)
        return (grad_in, buffer, sum_first, sum_second)

    start = (
        jnp.zeros(local_inputs.shape[1:], jnp.bfloat16),
        jnp.zeros(local_inputs.shape, jnp.bfloat16),
        jnp.zeros(first_weights.shape, jnp.float32),
        jnp.zeros(second_weights.shape, jnp.float32),
    )
    step_count = micro_count + section_count - 1
    outgoing, buffer, sum_first, sum_second = lax.fori_loop(0, step_count, advance, start)
    return (buffer[None], sum_first[None], sum_second[None])


def solution(mesh):
    placed = (
        P("pipe", None, None, "tensor"),
        P(None, None, "tensor"),
        P("pipe", None, "tensor", None, None),
        P("pipe", None, "tensor", None, None),
        P("pipe", None),
        P("pipe", None, None),
    )
    return jax.shard_map(
        on_device,
        mesh=mesh,
        in_specs=placed,
        out_specs=(
            P("pipe", None, None, "tensor"),
            P("pipe", None, "tensor", None, None),
            P("pipe", None, "tensor", None, None),
        ),
        check_vma=False,
    )
```

profile of v0, /device:TPU:0, one launch (start us, length us, event | category | flops | bytes accessed | tf_op | source)
XLA Modules:
  0.0 1600.5 jit_solution(7308023038977270801)
XLA Ops:
  32.4 26.4 %gather_fusion.4 = s32[3072]{0:T(1024)S(1)} fusion(s32[4,3072]{1,0:T(4,128)S(1)} %reshape_squeeze.3, s32[3072]{0:T(1024)S(1)} %reshape.172), kind=kCustom, calls=%fused_computation.4 | custom fusion | bytes 49152 | tf_op jit(solution)/shard_map/jit(take_along_axis)/gather | solution.py:67
  68.8 1524.8 %while.22 = (s32[]{:T(128)}, bf16[128,3072]{0,1:T(8,128)(2,1)}, bf16[8,128,3072]{2,1,0:T(8,128)(2,1)}, f32[1,24,128,128]{3,2,1,0:T(8,128)}, f32[1,24,128,128]{3,...) while((s32[]{:T(128)}, bf16[128,3072]{0,1:T(8,128)(2,1)}, ...), condition=%wide.region_5.7_spmd.clone, body=%wide.region_4.6_spmd.clone.sunk | while | flops 520347648 | bytes 93020776 | solution.py:170
  77.2 11.4 gather_fusion
  105.2 11.4 gather_fusion.1
  119.7 11.4 gather_fusion.2
  147.6 9.2 gather_fusion.3
  174.7 11.4 gather_fusion
  201.3 11.4 gather_fusion.1
  215.9 11.4 gather_fusion.2
  265.6 11.7 collective-permute-done
  279.0 11.4 gather_fusion
  305.7 11.4 gather_fusion.1
  320.3 11.4 gather_fusion.2
  349.6 9.2 gather_fusion.3
  369.9 9.9 collective-permute-done
  381.7 11.4 gather_fusion
  408.3 11.4 gather_fusion.1
  422.9 11.4 gather_fusion.2
  472.5 9.9 collective-permute-done
  484.3 11.4 gather_fusion
  510.9 11.4 gather_fusion.1
  525.5 11.4 gather_fusion.2
  575.1 9.9 collective-permute-done
  586.9 11.4 gather_fusion
  613.5 11.4 gather_fusion.1
  628.1 11.4 gather_fusion.2
  677.8 9.9 collective-permute-done
  689.5 11.4 gather_fusion
  716.1 11.4 gather_fusion.1
  730.7 11.4 gather_fusion.2
  780.4 9.9 collective-permute-done
  792.1 11.4 gather_fusion
  818.7 11.4 gather_fusion.1
  833.3 11.4 gather_fusion.2
  883.0 9.9 collective-permute-done
  894.7 11.4 gather_fusion
  921.3 11.4 gather_fusion.1
  935.9 11.4 gather_fusion.2
  985.6 9.9 collective-permute-done
  997.3 11.4 gather_fusion
  1024.0 11.4 gather_fusion.1
  1038.5 11.4 gather_fusion.2
  1067.9 9.2 gather_fusion.3
  1088.2 9.9 collective-permute-done
  1099.9 11.4 gather_fusion
  1126.6 11.4 gather_fusion.1
  1141.1 11.4 gather_fusion.2
  1190.8 9.9 collective-permute-done
  1202.5 11.4 gather_fusion
  1229.2 11.4 gather_fusion.1
  1243.7 11.4 gather_fusion.2
  1293.4 9.9 collective-permute-done
  1305.1 11.4 gather_fusion
  1331.8 11.4 gather_fusion.1
  1346.3 11.4 gather_fusion.2
  1375.7 9.2 gather_fusion.3
  1396.0 9.9 collective-permute-done
  1407.7 11.4 gather_fusion
  1434.4 11.4 gather_fusion.1
  1448.9 11.4 gather_fusion.2
  1498.6 9.9 collective-permute-done
  1510.3 11.4 gather_fusion
  1537.0 11.4 gather_fusion.1
  1551.5 11.4 gather_fusion.2
  (718 shorter events, 873.9 us)
Async XLA Ops:
  7.2 24.5 %sort.67.cloned.1.call-start = ((), (), s32[]{:S(2)}) async-start(), calls=%async_computation.2 | async-start | bytes 294944 | tf_op jit(solution)/shard_map/jit(argsort)/sort | solution.py:65
  69.8 5.6 collective-permute-start
  92.0 13.2 all-to-all-start
  134.5 13.1 all-to-all-start.1
  162.4 10.5 collective-permute-start
  189.4 11.9 all-to-all-start
  230.6 14.6 all-to-all-start.1
  260.0 17.3 %collective-permute-start = (bf16[128,3072]{0,1:T(8,128)(2,1)}, bf16[128,3072]{0,1:T(8,128)(2,1)}, u32[]{:S(2)}, u32[]{:S(2)}) collective-permute-start(bf16[128,3072]{0,1:T(8,128)(2,1)} %broadcast_select_fusion.8), channel_id=1, source_target_pairs={{4,0},{8,4},{12,8},{16,12},{20,16},{24,20},{28,24},{5,1},{9,5},{13... | collective-permute-start | bytes 2359304 | tf_op jit(solution)/shard_map/while/body/eval_jaxpr/ppermute | solution.py:13
  264.1 14.6 copy-start
  265.6 13.1 copy-start.8
  293.8 11.9 all-to-all-start
  335.0 14.6 all-to-all-start.1
  364.4 15.5 collective-permute-start
  368.4 12.8 copy-start
  369.9 11.4 copy-start.8
  396.4 11.9 all-to-all-start
  437.6 14.6 all-to-all-start.1
  467.0 15.5 collective-permute-start
  471.0 12.8 copy-start
  472.5 11.4 copy-start.8
  499.0 11.9 all-to-all-start
  540.2 14.6 all-to-all-start.1
  569.6 15.5 collective-permute-start
  573.6 12.8 copy-start
  601.6 11.9 all-to-all-start
  642.8 14.6 all-to-all-start.1
  672.2 15.5 collective-permute-start
  676.3 12.8 copy-start
  704.2 11.9 all-to-all-start
  745.4 14.6 all-to-all-start.1
  774.8 15.5 collective-permute-start
  778.9 12.8 copy-start
  780.3 11.4 copy-start.8
  806.9 11.9 all-to-all-start
  848.0 14.6 all-to-all-start.1
  877.4 15.5 collective-permute-start
  881.5 12.8 copy-start
  909.4 11.9 all-to-all-start
  950.7 14.6 all-to-all-start.1
  980.0 15.5 collective-permute-start
  984.1 12.8 copy-start
  1012.1 11.9 all-to-all-start
  1053.3 14.6 all-to-all-start.1
  1082.6 15.5 collective-permute-start
  1086.7 12.8 copy-start
  1088.2 11.4 copy-start.8
  1114.7 11.9 all-to-all-start
  1155.9 14.6 all-to-all-start.1
  1185.2 15.5 collective-permute-start
  1189.3 12.8 copy-start
  1217.3 11.9 all-to-all-start
  1258.5 14.6 all-to-all-start.1
  1287.8 15.5 collective-permute-start
  1291.9 12.8 copy-start
  1319.9 11.9 all-to-all-start
  1361.1 14.6 all-to-all-start.1
  1390.5 15.5 collective-permute-start
  1394.5 12.8 copy-start
  1422.5 11.9 all-to-all-start
  1463.7 14.6 all-to-all-start.1
  1493.1 15.5 collective-permute-start
  1497.1 12.8 copy-start
  1525.1 11.9 all-to-all-start
  1566.3 14.6 all-to-all-start.1
  (103 other events, 280.2 us)
Sparse Core Ops, SparseCore 0:
  11.1 11.7 sort.69.cloned.1.call-done
  (1 shorter events, 0.0 us)
where the time goes:
time: 1620 us; the launch traced here: 1600 us
  local copies, waits for them, and re-layouts  855 us (53%)
  other arithmetic  286 us (18%)
  waiting for transfers between devices  198 us (12%)
  starting transfers between devices  131 us (8%)
  matrix products  112 us (7%)
    gather x15, local copies, waits for them, and re-layouts, mix_backward(): jnp.take(grad_mixed, arrival, axis=1)  172 us
    gather x15, local copies, waits for them, and re-layouts, mix_forward(): outgoing = jnp.take(hidden, send_index, axis=1)  171 us
    gather x15, local copies, waits for them, and re-layouts, mix_backward(): return jnp.take(returned, gathering, axis=1)  171 us
    gather x15, local copies, waits for them, and re-layouts, mix_forward(): jnp.take(lax.all_to_all(outgoing, 'tensor', split_axis=1, concat_axis=1,...  137 us
    ppermute x15, waiting for transfers between devices, passed_along(): return lax.ppermute(block, axis, route)  136 us
    dynamic_slice x30, local copies, waits for them, and re-layouts, advance(): previous = lax.dynamic_index_in_dim(buffer, clipped, 0, keepdims=False)  69.9 us
    all_to_all x15, waiting for transfers between devices, mix_backward(): lax.all_to_all(jnp.take(grad_mixed, arrival, axis=1), 'tensor', split_axi...  61.9 us
    all_to_all x15, starting transfers between devices, mix_backward(): lax.all_to_all(jnp.take(grad_mixed, arrival, axis=1), 'tensor', split_axi...  59.3 us
  transfers between devices with their start and end apart: 45, of which 29 were waited for; matrix products, arithmetic and copies ran while one was open for 18% of the time, Pallas kernels for 0%

commit v1 on v0

v1 whole, which is shorter than its diff:
```python
import jax
import jax.numpy as jnp
from jax import lax
from jax.sharding import PartitionSpec as P

gelu_scale = 0.7978845608028654
gelu_cubic = 0.044715
LANES = 128


def gelu_both(values):
    square = values * values
    tangent = jnp.tanh(gelu_scale * (values + gelu_cubic * square * values))
    value = 0.5 * values * (1.0 + tangent)
    slope = 0.5 * (1.0 + tangent) + 0.5 * values * (1.0 - tangent * tangent) * gelu_scale * (
        1.0 + 3.0 * gelu_cubic * square
    )
    return value, slope


def block_product(values, weight, spec):
    count, size, _ = weight.shape
    split = values.reshape(values.shape[0], count, size)
    result = jnp.einsum(spec, split, weight, preferred_element_type=jnp.float32)
    return result.reshape(values.shape)


def block_outer(left, right, count):
    left_blocks = left.reshape(left.shape[0], count, -1)
    right_blocks = right.reshape(right.shape[0], count, -1)
    return jnp.einsum("tbi,tbj->bij", left_blocks, right_blocks, preferred_element_type=jnp.float32)


def running_rank(member):
    rows, width = member.shape
    tile = LANES
    pieces = member.reshape(rows, width // tile, tile).astype(jnp.bfloat16)
    upper = jnp.triu(jnp.ones((tile, tile), jnp.bfloat16))
    inner = jnp.einsum("rbi,ij->rbj", pieces, upper, preferred_element_type=jnp.float32)
    totals = inner[:, :, -1].astype(jnp.bfloat16)
    blocks = width // tile
    strict = jnp.triu(jnp.ones((blocks, blocks), jnp.bfloat16), 1)
    before = jnp.einsum("rb,bc->rc", totals, strict, preferred_element_type=jnp.float32)
    return (inner + before[:, :, None]).reshape(rows, width).astype(jnp.int32) - 1


def mixing(source_row, group_index, group_count):
    feat_count = source_row.shape[0] // group_count
    per_peer = feat_count // group_count
    slots = -(-per_peer // LANES) * LANES
    targets = source_row.reshape(group_count, feat_count)
    groups = targets // feat_count
    place = jnp.arange(slots, dtype=jnp.int32)

    mine = groups == group_index
    rank = jnp.where(mine, running_rank(mine), -1)
    feature = targets - group_index * feat_count
    hit = rank[:, None, :] == place[None, :, None]
    chosen = jnp.sum(jnp.where(hit, feature[:, None, :] + 1, 0), axis=2) - 1
    leaving = (chosen[:, :, None] == jnp.arange(feat_count, dtype=jnp.int32)).astype(jnp.bfloat16)

    own = lax.dynamic_index_in_dim(groups, group_index, 0, keepdims=False)
    member = own[None, :] == jnp.arange(group_count, dtype=jnp.int32)[:, None]
    own_rank = jnp.where(member, running_rank(member), -1)
    landing = (own_rank[:, None, :] == place[None, :, None]).astype(jnp.bfloat16)
    return leaving, landing


def exchange(values):
    return lax.all_to_all(values, "tensor", split_axis=0, concat_axis=0, tiled=True)


def relay(cotangents, slopes, back_mix, leaving, first_weights):
    section_count = lax.axis_size("pipe")
    section_index = lax.axis_index("pipe")
    micro_count = cotangents.shape[0]
    route = [(i, i - 1) for i in range(1, section_count)]

    def advance(step, carry):
        outgoing, grads, befores = carry
        incoming = lax.ppermute(outgoing, "pipe", route)
        micro = step - (section_count - 1 - section_index)
        live = (micro >= 0) & (micro < micro_count)
        micro = jnp.clip(micro, 0, micro_count - 1)
        last = lax.dynamic_index_in_dim(cotangents, micro, 0, keepdims=False)
        grad_now = jnp.where(section_index == section_count - 1, last, incoming)
        sent = jnp.einsum(
            "tj,hjk->htk", grad_now, back_mix, preferred_element_type=jnp.float32
        ).astype(jnp.bfloat16)
        came = exchange(sent)
        hidden = jnp.einsum("htk,hkf->tf", came, leaving, preferred_element_type=jnp.float32)
        slope = lax.dynamic_index_in_dim(slopes, micro, 0, keepdims=False)
        before = (hidden * slope.astype(jnp.float32)).astype(jnp.bfloat16)
        back = block_product(before, first_weights, "tbj,bij->tbi")
        grad = (grad_now.astype(jnp.float32) + back).astype(jnp.bfloat16)

        def keep(buffer, value):
            old = lax.dynamic_index_in_dim(buffer, micro, 0, keepdims=False)
            return lax.dynamic_update_index_in_dim(buffer, jnp.where(live, value, old), micro, 0)

        return grad, keep(grads, grad), keep(befores, before)

    empty = jnp.zeros(cotangents.shape, jnp.bfloat16)
    start = (jnp.zeros(cotangents.shape[1:], jnp.bfloat16), empty, empty)
    _, grads, befores = lax.fori_loop(0, micro_count + section_count - 1, advance, start)
    return grads, befores


def on_device(section_inputs, out_grad, w_first, w_second, drop_flags, perm):
    section_count = lax.axis_size("pipe")
    section_index = lax.axis_index("pipe")
    group_count = lax.axis_size("tensor")
    group_index = lax.axis_index("tensor")
    _, micro_count, token_count, feat_count = section_inputs.shape
    first_weights = w_first[0, 0]
    second_weights = w_second[0, 0]
    block_count, size, _ = first_weights.shape
    kept = drop_flags[0, 0].astype(jnp.bfloat16)
    leaving, landing = mixing(perm[0, 0], group_index, group_count)
    slots = leaving.shape[1]

    inputs = section_inputs[0].reshape(-1, feat_count)
    before = block_product(inputs, first_weights, "tbi,bij->tbj")
    hidden, slopes = gelu_both(before)
    sent = jnp.einsum(
        "tf,hkf->htk", hidden.astype(jnp.bfloat16), leaving, preferred_element_type=jnp.float32
    ).astype(jnp.bfloat16)
    came = exchange(sent)
    mixed = jnp.einsum(
        "qtk,qkp->tp", came, landing, preferred_element_type=jnp.float32
    ).astype(jnp.bfloat16)

    back_mix = jnp.einsum(
        "bij,qkbi->qbjk",
        second_weights * kept,
        landing.reshape(group_count, slots, block_count, size),
        preferred_element_type=jnp.float32,
    ).astype(jnp.bfloat16).reshape(group_count, feat_count, slots)

    chunked = (micro_count, token_count, feat_count)
    grads, befores = relay(
        out_grad, slopes.astype(jnp.bfloat16).reshape(chunked), back_mix, leaving, first_weights
    )
    arrived = lax.ppermute(grads, "pipe", [(i, i - 1) for i in range(1, section_count)])
    cotangent = jnp.where(section_index == section_count - 1, out_grad, arrived)
    branch = cotangent.reshape(-1, feat_count) * kept
    second_grad = block_outer(mixed, branch, block_count)
    first_grad = block_outer(inputs, befores.reshape(-1, feat_count), block_count)
    return grads[None], first_grad[None, None], second_grad[None, None]


def solution(mesh):
    placed = (
        P("pipe", None, None, "tensor"),
        P(None, None, "tensor"),
        P("pipe", None, "tensor", None, None),
        P("pipe", None, "tensor", None, None),
        P("pipe", None),
        P("pipe", None, None),
    )
    return jax.shard_map(
        on_device,
        mesh=mesh,
        in_specs=placed,
        out_specs=(
            P("pipe", None, None, "tensor"),
            P("pipe", None, "tensor", None, None),
            P("pipe", None, "tensor", None, None),
        ),
        check_vma=False,
    )
```

time: 1620 us -> 992 us (0.61)
  the two profiles are of different devices: /device:TPU:0 before, /device:TPU:17 now
where the time goes in v1:
time: 992 us; the launch traced here: 978 us
  matrix products  357 us (36%)
  waiting for transfers between devices  331 us (33%)
  local copies, waits for them, and re-layouts  129 us (13%)
  starting transfers between devices  89.3 us (9%)
  other arithmetic  69.3 us (7%)
    ppermute x15, waiting for transfers between devices, advance(): incoming = lax.ppermute(outgoing, 'pipe', route)  170 us
    all_to_all x16, waiting for transfers between devices, exchange(): lax.all_to_all(values, 'tensor', split_axis=0, concat_axis=0, tiled=True)  161 us
    dot_general x15, matrix products, advance(): jnp.einsum('tj,hjk->htk', grad_now, back_mix, preferred_element_type=jnp....  156 us
    dot_general x15, matrix products, advance(): jnp.einsum('htk,hkf->tf', came, leaving, preferred_element_type=jnp.float32)  78.9 us
    all_to_all x16, starting transfers between devices, exchange(): lax.all_to_all(values, 'tensor', split_axis=0, concat_axis=0, tiled=True)  57.8 us
    dynamic_update_slice x15, other arithmetic, keep(): lax.dynamic_update_index_in_dim(buffer, jnp.where(live, value, old), micr...  45.1 us
    dot_general x1, matrix products, on_device(): jnp.einsum('qtk,qkp->tp', came, landing, preferred_element_type=jnp.float32)  37.1 us
    dynamic_slice x15, local copies, waits for them, and re-layouts, keep(): old = lax.dynamic_index_in_dim(buffer, micro, 0, keepdims=False)  35.4 us
  transfers between devices with their start and end apart: 32, of which 31 were waited for; matrix products, arithmetic and copies ran while one was open for 10% of the time, Pallas kernels for 0%

profile of v1, /device:TPU:17, one launch (start us, length us, event | category | flops | bytes accessed | tf_op | source)
XLA Modules:
  0.0 978.2 jit_solution(7125987147844488745)
XLA Ops:
  16.4 8.1 fusion.44
  24.5 12.5 %copy.74 = f32[384,8,8,128]{3,2,1,0:T(8,128)} copy(f32[384,8,8,128]{3,1,2,0:T(8,128)} %bitcast.144) | data formatting | bytes 25165824
  37.0 12.7 %copy.52 = f32[8,128,3072]{2,1,0:T(8,128)} copy(f32[8,128,3072]{1,0,2:T(8,128)} %bitcast.146) | data formatting | bytes 25165824 | tf_op jit(solution)/shard_map/reshape | solution.py:25
  49.7 11.3 %add_convert_fusion.1 = bf16[8,128,3072]{2,1,0:T(8,128)(2,1)} fusion(f32[8,128,3072]{2,1,0:T(8,128)} %copy.52), kind=kLoop, calls=%fused_computation.46 | loop fusion | flops 53477376 | bytes 18874368 | tf_op jit(solution)/shard_map/convert_element_type | solution.py:142
  61.0 12.6 %copy.56 = f32[1024,3072]{1,0:T(8,128)} copy(f32[1024,3072]{0,1:T(8,128)} %bitcast.145) | data formatting | bytes 25165824 | tf_op jit(solution)/shard_map/reshape | solution.py:25
  73.6 11.7 %convert_bitcast_fusion = bf16[4,24,128,768]{3,2,0,1:T(8,128)(2,1)} fusion(s32[4,24,128]{2,0,1:T(4,128)S(1)} %copy.44, bf16[1,1,24,128,128]{4,3,2,1,0:T(8,128)(2,1)S(1)} %copy-done.6, bf16[]{:T(256)} %bitcast.2), kind=kOutput, calls=%fused_computation.36 | convolution fusion | flops 2435186688 | bytes 19709954 | tf_op jit(solution)/shard_map/bij,qkbi->qbjk/dot_general | solution.py:133
  85.3 17.0 %copy.46 = bf16[4,24,128,768]{3,2,1,0:T(8,128)(2,1)} copy(bf16[4,24,128,768]{3,2,0,1:T(8,128)(2,1)} %convert_bitcast_fusion) | data formatting | bytes 37748736 | tf_op jit(solution)/shard_map/convert_element_type | solution.py:138
  102.3 28.7 %convert_bitcast_fusion.1 = bf16[4,1024,768]{1,2,0:T(8,128)(2,1)} fusion(f32[1024,3072]{1,0:T(8,128)} %copy.56, s32[4,768]{1,0:T(4,128)S(1)} %broadcast_add_fusion), kind=kOutput, calls=%fused_computation.53 | convolution fusion | flops 19368247296 | bytes 18886656 | tf_op jit(solution)/shard_map/tf,hkf->htk/dot_general | solution.py:125
  138.0 708.0 %while.20 = (s32[]{:T(128)}, bf16[128,3072]{1,0:T(8,128)(2,1)S(1)}, bf16[8,128,3072]{2,1,0:T(8,128)(2,1)}, bf16[8,128,3072]{2,1,0:T(8,128)(2,1)}, pred[]{:T(512)...) while((s32[]{:T(128)}, bf16[128,3072]{1,0:T(8,128)(2,1)S(1)}, ...), condition=%wide.region_2.3_spmd.clone, body=%wide.region_1.2_spmd.clone.sunk | while | flops 4956094464 | bytes 50345284 | solution.py:105
  140.7 10.8 %collective-permute-done = bf16[128,3072]{1,0:T(8,128)(2,1)S(1)} collective-permute-done((bf16[128,3072]{1,0:T(8,128)(2,1)S(1)}, bf16[128,3072]{1,0:T(8,128)(2,1)S(1)}, u32[]{:S(2)}, u32[]{:S(2)}) %collective-permute-start) | collective-permute-done | bytes 786464 | tf_op jit(solution)/shard_map/while/body/eval_jaxpr/ppermute | solution.py:81
  151.5 10.4 %fusion.126 = bf16[4,128,768]{2,1,0:T(8,128)(2,1)} fusion(bf16[4,3072,768]{2,1,0:T(8,128)(2,1)} %get-tuple-element.443, bf16[128,3072]{1,0:T(8,128)(2,1)S(1)} %collective-permute-done, bf16[8,128,3072]{2,1,0:T(8,128)(2,1)} %get-tuple-element.442, s32[]{:T(128)S(6)} %min.12, pred[]{:T(512)} %get-tuple-element.440), kind=kOutput, calls=%fused_computation.10.clone.1 | convolution fusion | flops 2416705536 | bytes 21234180 | tf_op jit(solution)/shard_map/while/body/eval_jaxpr/tj,hjk->htk/dot_general | solution.py:87
  167.8 8.1 all-to-all-done
  175.8 5.3 bitcast_dynamic-update-slice_fusion.4
  188.5 11.3 %collective-permute-done = bf16[128,3072]{1,0:T(8,128)(2,1)S(1)} collective-permute-done((bf16[128,3072]{1,0:T(8,128)(2,1)S(1)}, bf16[128,3072]{1,0:T(8,128)(2,1)S(1)}, u32[]{:S(2)}, u32[]{:S(2)}) %collective-permute-start) | collective-permute-done | bytes 786464 | tf_op jit(solution)/shard_map/while/body/eval_jaxpr/ppermute | solution.py:81
  199.8 10.4 %fusion.126 = bf16[4,128,768]{2,1,0:T(8,128)(2,1)} fusion(bf16[4,3072,768]{2,1,0:T(8,128)(2,1)} %get-tuple-element.443, bf16[128,3072]{1,0:T(8,128)(2,1)S(1)} %collective-permute-done, bf16[8,128,3072]{2,1,0:T(8,128)(2,1)} %get-tuple-element.442, s32[]{:T(128)S(6)} %min.12, pred[]{:T(512)} %get-tuple-element.440), kind=kOutput, calls=%fused_computation.10.clone.1 | convolution fusion | flops 2416705536 | bytes 21234180 | tf_op jit(solution)/shard_map/while/body/eval_jaxpr/tj,hjk->htk/dot_general | solution.py:87
  216.0 7.8 all-to-all-done
  223.8 5.3 bitcast_dynamic-update-slice_fusion.4
  236.4 11.4 %collective-permute-done = bf16[128,3072]{1,0:T(8,128)(2,1)S(1)} collective-permute-done((bf16[128,3072]{1,0:T(8,128)(2,1)S(1)}, bf16[128,3072]{1,0:T(8,128)(2,1)S(1)}, u32[]{:S(2)}, u32[]{:S(2)}) %collective-permute-start) | collective-permute-done | bytes 786464 | tf_op jit(solution)/shard_map/while/body/eval_jaxpr/ppermute | solution.py:81
  247.8 10.4 %fusion.126 = bf16[4,128,768]{2,1,0:T(8,128)(2,1)} fusion(bf16[4,3072,768]{2,1,0:T(8,128)(2,1)} %get-tuple-element.443, bf16[128,3072]{1,0:T(8,128)(2,1)S(1)} %collective-permute-done, bf16[8,128,3072]{2,1,0:T(8,128)(2,1)} %get-tuple-element.442, s32[]{:T(128)S(6)} %min.12, pred[]{:T(512)} %get-tuple-element.440), kind=kOutput, calls=%fused_computation.10.clone.1 | convolution fusion | flops 2416705536 | bytes 21234180 | tf_op jit(solution)/shard_map/while/body/eval_jaxpr/tj,hjk->htk/dot_general | solution.py:87
  264.0 7.3 all-to-all-done
  271.4 5.3 bitcast_dynamic-update-slice_fusion.4
  284.0 11.4 %collective-permute-done = bf16[128,3072]{1,0:T(8,128)(2,1)S(1)} collective-permute-done((bf16[128,3072]{1,0:T(8,128)(2,1)S(1)}, bf16[128,3072]{1,0:T(8,128)(2,1)S(1)}, u32[]{:S(2)}, u32[]{:S(2)}) %collective-permute-start) | collective-permute-done | bytes 786464 | tf_op jit(solution)/shard_map/while/body/eval_jaxpr/ppermute | solution.py:81
  295.3 10.4 %fusion.126 = bf16[4,128,768]{2,1,0:T(8,128)(2,1)} fusion(bf16[4,3072,768]{2,1,0:T(8,128)(2,1)} %get-tuple-element.443, bf16[128,3072]{1,0:T(8,128)(2,1)S(1)} %collective-permute-done, bf16[8,128,3072]{2,1,0:T(8,128)(2,1)} %get-tuple-element.442, s32[]{:T(128)S(6)} %min.12, pred[]{:T(512)} %get-tuple-element.440), kind=kOutput, calls=%fused_computation.10.clone.1 | convolution fusion | flops 2416705536 | bytes 21234180 | tf_op jit(solution)/shard_map/while/body/eval_jaxpr/tj,hjk->htk/dot_general | solution.py:87
  311.6 6.8 all-to-all-done
  330.9 11.4 %collective-permute-done = bf16[128,3072]{1,0:T(8,128)(2,1)S(1)} collective-permute-done((bf16[128,3072]{1,0:T(8,128)(2,1)S(1)}, bf16[128,3072]{1,0:T(8,128)(2,1)S(1)}, u32[]{:S(2)}, u32[]{:S(2)}) %collective-permute-start) | collective-permute-done | bytes 786464 | tf_op jit(solution)/shard_map/while/body/eval_jaxpr/ppermute | solution.py:81
  342.3 10.4 %fusion.126 = bf16[4,128,768]{2,1,0:T(8,128)(2,1)} fusion(bf16[4,3072,768]{2,1,0:T(8,128)(2,1)} %get-tuple-element.443, bf16[128,3072]{1,0:T(8,128)(2,1)S(1)} %collective-permute-done, bf16[8,128,3072]{2,1,0:T(8,128)(2,1)} %get-tuple-element.442, s32[]{:T(128)S(6)} %min.12, pred[]{:T(512)} %get-tuple-element.440), kind=kOutput, calls=%fused_computation.10.clone.1 | convolution fusion | flops 2416705536 | bytes 21234180 | tf_op jit(solution)/shard_map/while/body/eval_jaxpr/tj,hjk->htk/dot_general | solution.py:87
  358.6 6.9 all-to-all-done
  365.5 5.3 bitcast_dynamic-update-slice_fusion.4
  378.0 11.4 %collective-permute-done = bf16[128,3072]{1,0:T(8,128)(2,1)S(1)} collective-permute-done((bf16[128,3072]{1,0:T(8,128)(2,1)S(1)}, bf16[128,3072]{1,0:T(8,128)(2,1)S(1)}, u32[]{:S(2)}, u32[]{:S(2)}) %collective-permute-start) | collective-permute-done | bytes 786464 | tf_op jit(solution)/shard_map/while/body/eval_jaxpr/ppermute | solution.py:81
  389.4 10.4 %fusion.126 = bf16[4,128,768]{2,1,0:T(8,128)(2,1)} fusion(bf16[4,3072,768]{2,1,0:T(8,128)(2,1)} %get-tuple-element.443, bf16[128,3072]{1,0:T(8,128)(2,1)S(1)} %collective-permute-done, bf16[8,128,3072]{2,1,0:T(8,128)(2,1)} %get-tuple-element.442, s32[]{:T(128)S(6)} %min.12, pred[]{:T(512)} %get-tuple-element.440), kind=kOutput, calls=%fused_computation.10.clone.1 | convolution fusion | flops 2416705536 | bytes 21234180 | tf_op jit(solution)/shard_map/while/body/eval_jaxpr/tj,hjk->htk/dot_general | solution.py:87
  405.6 6.8 all-to-all-done
  425.0 11.4 %collective-permute-done = bf16[128,3072]{1,0:T(8,128)(2,1)S(1)} collective-permute-done((bf16[128,3072]{1,0:T(8,128)(2,1)S(1)}, bf16[128,3072]{1,0:T(8,128)(2,1)S(1)}, u32[]{:S(2)}, u32[]{:S(2)}) %collective-permute-start) | collective-permute-done | bytes 786464 | tf_op jit(solution)/shard_map/while/body/eval_jaxpr/ppermute | solution.py:81
  436.4 10.4 %fusion.126 = bf16[4,128,768]{2,1,0:T(8,128)(2,1)} fusion(bf16[4,3072,768]{2,1,0:T(8,128)(2,1)} %get-tuple-element.443, bf16[128,3072]{1,0:T(8,128)(2,1)S(1)} %collective-permute-done, bf16[8,128,3072]{2,1,0:T(8,128)(2,1)} %get-tuple-element.442, s32[]{:T(128)S(6)} %min.12, pred[]{:T(512)} %get-tuple-element.440), kind=kOutput, calls=%fused_computation.10.clone.1 | convolution fusion | flops 2416705536 | bytes 21234180 | tf_op jit(solution)/shard_map/while/body/eval_jaxpr/tj,hjk->htk/dot_general | solution.py:87
  452.6 6.9 all-to-all-done
  472.0 11.4 %collective-permute-done = bf16[128,3072]{1,0:T(8,128)(2,1)S(1)} collective-permute-done((bf16[128,3072]{1,0:T(8,128)(2,1)S(1)}, bf16[128,3072]{1,0:T(8,128)(2,1)S(1)}, u32[]{:S(2)}, u32[]{:S(2)}) %collective-permute-start) | collective-permute-done | bytes 786464 | tf_op jit(solution)/shard_map/while/body/eval_jaxpr/ppermute | solution.py:81
  483.4 10.4 %fusion.126 = bf16[4,128,768]{2,1,0:T(8,128)(2,1)} fusion(bf16[4,3072,768]{2,1,0:T(8,128)(2,1)} %get-tuple-element.443, bf16[128,3072]{1,0:T(8,128)(2,1)S(1)} %collective-permute-done, bf16[8,128,3072]{2,1,0:T(8,128)(2,1)} %get-tuple-element.442, s32[]{:T(128)S(6)} %min.12, pred[]{:T(512)} %get-tuple-element.440), kind=kOutput, calls=%fused_computation.10.clone.1 | convolution fusion | flops 2416705536 | bytes 21234180 | tf_op jit(solution)/shard_map/while/body/eval_jaxpr/tj,hjk->htk/dot_general | solution.py:87
  499.6 6.9 all-to-all-done
  506.5 5.3 bitcast_dynamic-update-slice_fusion.4
  519.1 11.4 %collective-permute-done = bf16[128,3072]{1,0:T(8,128)(2,1)S(1)} collective-permute-done((bf16[128,3072]{1,0:T(8,128)(2,1)S(1)}, bf16[128,3072]{1,0:T(8,128)(2,1)S(1)}, u32[]{:S(2)}, u32[]{:S(2)}) %collective-permute-start) | collective-permute-done | bytes 786464 | tf_op jit(solution)/shard_map/while/body/eval_jaxpr/ppermute | solution.py:81
  530.5 10.4 %fusion.126 = bf16[4,128,768]{2,1,0:T(8,128)(2,1)} fusion(bf16[4,3072,768]{2,1,0:T(8,128)(2,1)} %get-tuple-element.443, bf16[128,3072]{1,0:T(8,128)(2,1)S(1)} %collective-permute-done, bf16[8,128,3072]{2,1,0:T(8,128)(2,1)} %get-tuple-element.442, s32[]{:T(128)S(6)} %min.12, pred[]{:T(512)} %get-tuple-element.440), kind=kOutput, calls=%fused_computation.10.clone.1 | convolution fusion | flops 2416705536 | bytes 21234180 | tf_op jit(solution)/shard_map/while/body/eval_jaxpr/tj,hjk->htk/dot_general | solution.py:87
  546.7 6.8 all-to-all-done
  553.5 5.3 bitcast_dynamic-update-slice_fusion.4
  566.0 11.4 %collective-permute-done = bf16[128,3072]{1,0:T(8,128)(2,1)S(1)} collective-permute-done((bf16[128,3072]{1,0:T(8,128)(2,1)S(1)}, bf16[128,3072]{1,0:T(8,128)(2,1)S(1)}, u32[]{:S(2)}, u32[]{:S(2)}) %collective-permute-start) | collective-permute-done | bytes 786464 | tf_op jit(solution)/shard_map/while/body/eval_jaxpr/ppermute | solution.py:81
  577.4 10.4 %fusion.126 = bf16[4,128,768]{2,1,0:T(8,128)(2,1)} fusion(bf16[4,3072,768]{2,1,0:T(8,128)(2,1)} %get-tuple-element.443, bf16[128,3072]{1,0:T(8,128)(2,1)S(1)} %collective-permute-done, bf16[8,128,3072]{2,1,0:T(8,128)(2,1)} %get-tuple-element.442, s32[]{:T(128)S(6)} %min.12, pred[]{:T(512)} %get-tuple-element.440), kind=kOutput, calls=%fused_computation.10.clone.1 | convolution fusion | flops 2416705536 | bytes 21234180 | tf_op jit(solution)/shard_map/while/body/eval_jaxpr/tj,hjk->htk/dot_general | solution.py:87
  593.7 6.8 all-to-all-done
  613.0 11.4 %collective-permute-done = bf16[128,3072]{1,0:T(8,128)(2,1)S(1)} collective-permute-done((bf16[128,3072]{1,0:T(8,128)(2,1)S(1)}, bf16[128,3072]{1,0:T(8,128)(2,1)S(1)}, u32[]{:S(2)}, u32[]{:S(2)}) %collective-permute-start) | collective-permute-done | bytes 786464 | tf_op jit(solution)/shard_map/while/body/eval_jaxpr/ppermute | solution.py:81
  624.4 10.4 %fusion.126 = bf16[4,128,768]{2,1,0:T(8,128)(2,1)} fusion(bf16[4,3072,768]{2,1,0:T(8,128)(2,1)} %get-tuple-element.443, bf16[128,3072]{1,0:T(8,128)(2,1)S(1)} %collective-permute-done, bf16[8,128,3072]{2,1,0:T(8,128)(2,1)} %get-tuple-element.442, s32[]{:T(128)S(6)} %min.12, pred[]{:T(512)} %get-tuple-element.440), kind=kOutput, calls=%fused_computation.10.clone.1 | convolution fusion | flops 2416705536 | bytes 21234180 | tf_op jit(solution)/shard_map/while/body/eval_jaxpr/tj,hjk->htk/dot_general | solution.py:87
  640.7 6.8 all-to-all-done
  660.0 11.4 %collective-permute-done = bf16[128,3072]{1,0:T(8,128)(2,1)S(1)} collective-permute-done((bf16[128,3072]{1,0:T(8,128)(2,1)S(1)}, bf16[128,3072]{1,0:T(8,128)(2,1)S(1)}, u32[]{:S(2)}, u32[]{:S(2)}) %collective-permute-start) | collective-permute-done | bytes 786464 | tf_op jit(solution)/shard_map/while/body/eval_jaxpr/ppermute | solution.py:81
  671.4 10.4 %fusion.126 = bf16[4,128,768]{2,1,0:T(8,128)(2,1)} fusion(bf16[4,3072,768]{2,1,0:T(8,128)(2,1)} %get-tuple-element.443, bf16[128,3072]{1,0:T(8,128)(2,1)S(1)} %collective-permute-done, bf16[8,128,3072]{2,1,0:T(8,128)(2,1)} %get-tuple-element.442, s32[]{:T(128)S(6)} %min.12, pred[]{:T(512)} %get-tuple-element.440), kind=kOutput, calls=%fused_computation.10.clone.1 | convolution fusion | flops 2416705536 | bytes 21234180 | tf_op jit(solution)/shard_map/while/body/eval_jaxpr/tj,hjk->htk/dot_general | solution.py:87
  687.7 6.8 all-to-all-done
  707.0 11.4 %collective-permute-done = bf16[128,3072]{1,0:T(8,128)(2,1)S(1)} collective-permute-done((bf16[128,3072]{1,0:T(8,128)(2,1)S(1)}, bf16[128,3072]{1,0:T(8,128)(2,1)S(1)}, u32[]{:S(2)}, u32[]{:S(2)}) %collective-permute-start) | collective-permute-done | bytes 786464 | tf_op jit(solution)/shard_map/while/body/eval_jaxpr/ppermute | solution.py:81
  718.4 10.4 %fusion.126 = bf16[4,128,768]{2,1,0:T(8,128)(2,1)} fusion(bf16[4,3072,768]{2,1,0:T(8,128)(2,1)} %get-tuple-element.443, bf16[128,3072]{1,0:T(8,128)(2,1)S(1)} %collective-permute-done, bf16[8,128,3072]{2,1,0:T(8,128)(2,1)} %get-tuple-element.442, s32[]{:T(128)S(6)} %min.12, pred[]{:T(512)} %get-tuple-element.440), kind=kOutput, calls=%fused_computation.10.clone.1 | convolution fusion | flops 2416705536 | bytes 21234180 | tf_op jit(solution)/shard_map/while/body/eval_jaxpr/tj,hjk->htk/dot_general | solution.py:87
  734.7 6.8 all-to-all-done
  754.0 11.4 %collective-permute-done = bf16[128,3072]{1,0:T(8,128)(2,1)S(1)} collective-permute-done((bf16[128,3072]{1,0:T(8,128)(2,1)S(1)}, bf16[128,3072]{1,0:T(8,128)(2,1)S(1)}, u32[]{:S(2)}, u32[]{:S(2)}) %collective-permute-start) | collective-permute-done | bytes 786464 | tf_op jit(solution)/shard_map/while/body/eval_jaxpr/ppermute | solution.py:81
  765.4 10.4 %fusion.126 = bf16[4,128,768]{2,1,0:T(8,128)(2,1)} fusion(bf16[4,3072,768]{2,1,0:T(8,128)(2,1)} %get-tuple-element.443, bf16[128,3072]{1,0:T(8,128)(2,1)S(1)} %collective-permute-done, bf16[8,128,3072]{2,1,0:T(8,128)(2,1)} %get-tuple-element.442, s32[]{:T(128)S(6)} %min.12, pred[]{:T(512)} %get-tuple-element.440), kind=kOutput, calls=%fused_computation.10.clone.1 | convolution fusion | flops 2416705536 | bytes 21234180 | tf_op jit(solution)/shard_map/while/body/eval_jaxpr/tj,hjk->htk/dot_general | solution.py:87
  781.6 6.8 all-to-all-done
  801.0 11.4 %collective-permute-done = bf16[128,3072]{1,0:T(8,128)(2,1)S(1)} collective-permute-done((bf16[128,3072]{1,0:T(8,128)(2,1)S(1)}, bf16[128,3072]{1,0:T(8,128)(2,1)S(1)}, u32[]{:S(2)}, u32[]{:S(2)}) %collective-permute-start) | collective-permute-done | bytes 786464 | tf_op jit(solution)/shard_map/while/body/eval_jaxpr/ppermute | solution.py:81
  812.4 10.4 %fusion.126 = bf16[4,128,768]{2,1,0:T(8,128)(2,1)} fusion(bf16[4,3072,768]{2,1,0:T(8,128)(2,1)} %get-tuple-element.443, bf16[128,3072]{1,0:T(8,128)(2,1)S(1)} %collective-permute-done, bf16[8,128,3072]{2,1,0:T(8,128)(2,1)} %get-tuple-element.442, s32[]{:T(128)S(6)} %min.12, pred[]{:T(512)} %get-tuple-element.440), kind=kOutput, calls=%fused_computation.10.clone.1 | convolution fusion | flops 2416705536 | bytes 21234180 | tf_op jit(solution)/shard_map/while/body/eval_jaxpr/tj,hjk->htk/dot_general | solution.py:87
  828.6 6.8 all-to-all-done
  846.0 5.4 all-to-all-start.1
  866.5 55.2 %all-to-all-done.1 = bf16[4,1024,768]{1,2,0:T(8,128)(2,1)} async-done(((bf16[4,1024,768]{1,2,0:T(8,128)(2,1)}), bf16[4,1024,768]{1,2,0:T(8,128)(2,1)}, u32[]{:S(2)}, u32[]{:S(2)}) %all-to-all-start.1) | async-done | bytes 6291488 | tf_op jit(solution)/shard_map/all_to_all | solution.py:70
  921.8 37.1 %bitcast_convert_fusion = bf16[1024,3072]{1,0:T(8,128)(2,1)} fusion(bf16[4,1024,768]{1,2,0:T(8,128)(2,1)} %all-to-all-done.1, s32[4,3072]{1,0:T(4,128)S(1)} %bitcast_select_fusion.4), kind=kOutput, calls=%fused_computation.45 | convolution fusion | flops 19339935744 | bytes 12632064 | tf_op jit(solution)/shard_map/qtk,qkp->tp/dot_general | solution.py:129
  958.9 8.9 copy.70
  (194 shorter events, 291.6 us)
Async XLA Ops:
  5.5 1.2 copy-start.4
  16.4 8.1 copy-start.1
  61.0 12.7 %copy-start.6 = (bf16[1,1,24,128,128]{4,3,2,1,0:T(8,128)(2,1)S(1)}, bf16[1,1,24,128,128]{4,3,2,1,0:T(8,128)(2,1)}, u32[]{:S(2)}) copy-start(bf16[1,1,24,128,128]{4,3,2,1,0:T(8,128)(2,1)} %param.11) | copy-start | bytes 2359300
  138.1 13.4 %collective-permute-start = (bf16[128,3072]{1,0:T(8,128)(2,1)S(1)}, bf16[128,3072]{1,0:T(8,128)(2,1)S(1)}, u32[]{:S(2)}, u32[]{:S(2)}) collective-permute-start(bf16[128,3072]{1,0:T(8,128)(2,1)S(1)} %broadcast_select_fusion.2), channel_id=1, source_target_pairs={{4,0},{8,4},{12,8},{16,12},{20,16},{24,20},{28,24},{5,1},{9,5},{13... | collective-permute-start | bytes 2359304 | tf_op jit(solution)/shard_map/while/body/eval_jaxpr/ppermute | solution.py:81
  151.5 10.4 %copy-start = (bf16[128,3072]{1,0:T(8,128)(2,1)}, bf16[128,3072]{1,0:T(8,128)(2,1)S(1)}, u32[]{:S(2)}) copy-start(bf16[128,3072]{1,0:T(8,128)(2,1)S(1)} %collective-permute-done) | copy-start | bytes 2359300 | tf_op jit(solution)/shard_map/while
  161.9 13.9 %all-to-all-start = ((bf16[4,128,768]{2,1,0:T(8,128)(2,1)}), bf16[4,128,768]{2,1,0:T(8,128)(2,1)S(1)}, u32[]{:S(2)}, u32[]{:S(2)}) async-start(bf16[4,128,768]{2,1,0:T(8,128)(2,1)} %fusion.126), calls=%async_computation | async-start | bytes 1572864 | tf_op jit(solution)/shard_map/while/body/eval_jaxpr/all_to_all | solution.py:70
  186.4 13.3 %collective-permute-start = (bf16[128,3072]{1,0:T(8,128)(2,1)S(1)}, bf16[128,3072]{1,0:T(8,128)(2,1)S(1)}, u32[]{:S(2)}, u32[]{:S(2)}) collective-permute-start(bf16[128,3072]{1,0:T(8,128)(2,1)S(1)} %broadcast_select_fusion.2), channel_id=1, source_target_pairs={{4,0},{8,4},{12,8},{16,12},{20,16},{24,20},{28,24},{5,1},{9,5},{13... | collective-permute-start | bytes 2359304 | tf_op jit(solution)/shard_map/while/body/eval_jaxpr/ppermute | solution.py:81
  199.8 10.4 %copy-start = (bf16[128,3072]{1,0:T(8,128)(2,1)}, bf16[128,3072]{1,0:T(8,128)(2,1)S(1)}, u32[]{:S(2)}) copy-start(bf16[128,3072]{1,0:T(8,128)(2,1)S(1)} %collective-permute-done) | copy-start | bytes 2359300 | tf_op jit(solution)/shard_map/while
  210.1 13.7 %all-to-all-start = ((bf16[4,128,768]{2,1,0:T(8,128)(2,1)}), bf16[4,128,768]{2,1,0:T(8,128)(2,1)S(1)}, u32[]{:S(2)}, u32[]{:S(2)}) async-start(bf16[4,128,768]{2,1,0:T(8,128)(2,1)} %fusion.126), calls=%async_computation | async-start | bytes 1572864 | tf_op jit(solution)/shard_map/while/body/eval_jaxpr/all_to_all | solution.py:70
  234.5 13.3 %collective-permute-start = (bf16[128,3072]{1,0:T(8,128)(2,1)S(1)}, bf16[128,3072]{1,0:T(8,128)(2,1)S(1)}, u32[]{:S(2)}, u32[]{:S(2)}) collective-permute-start(bf16[128,3072]{1,0:T(8,128)(2,1)S(1)} %broadcast_select_fusion.2), channel_id=1, source_target_pairs={{4,0},{8,4},{12,8},{16,12},{20,16},{24,20},{28,24},{5,1},{9,5},{13... | collective-permute-start | bytes 2359304 | tf_op jit(solution)/shard_map/while/body/eval_jaxpr/ppermute | solution.py:81
  247.8 10.4 %copy-start = (bf16[128,3072]{1,0:T(8,128)(2,1)}, bf16[128,3072]{1,0:T(8,128)(2,1)S(1)}, u32[]{:S(2)}) copy-start(bf16[128,3072]{1,0:T(8,128)(2,1)S(1)} %collective-permute-done) | copy-start | bytes 2359300 | tf_op jit(solution)/shard_map/while
  258.2 13.2 %all-to-all-start = ((bf16[4,128,768]{2,1,0:T(8,128)(2,1)}), bf16[4,128,768]{2,1,0:T(8,128)(2,1)S(1)}, u32[]{:S(2)}, u32[]{:S(2)}) async-start(bf16[4,128,768]{2,1,0:T(8,128)(2,1)} %fusion.126), calls=%async_computation | async-start | bytes 1572864 | tf_op jit(solution)/shard_map/while/body/eval_jaxpr/all_to_all | solution.py:70
  282.0 13.3 %collective-permute-start = (bf16[128,3072]{1,0:T(8,128)(2,1)S(1)}, bf16[128,3072]{1,0:T(8,128)(2,1)S(1)}, u32[]{:S(2)}, u32[]{:S(2)}) collective-permute-start(bf16[128,3072]{1,0:T(8,128)(2,1)S(1)} %broadcast_select_fusion.2), channel_id=1, source_target_pairs={{4,0},{8,4},{12,8},{16,12},{20,16},{24,20},{28,24},{5,1},{9,5},{13... | collective-permute-start | bytes 2359304 | tf_op jit(solution)/shard_map/while/body/eval_jaxpr/ppermute | solution.py:81
  295.3 10.4 %copy-start = (bf16[128,3072]{1,0:T(8,128)(2,1)}, bf16[128,3072]{1,0:T(8,128)(2,1)S(1)}, u32[]{:S(2)}) copy-start(bf16[128,3072]{1,0:T(8,128)(2,1)S(1)} %collective-permute-done) | copy-start | bytes 2359300 | tf_op jit(solution)/shard_map/while
  305.7 12.7 %all-to-all-start = ((bf16[4,128,768]{2,1,0:T(8,128)(2,1)}), bf16[4,128,768]{2,1,0:T(8,128)(2,1)S(1)}, u32[]{:S(2)}, u32[]{:S(2)}) async-start(bf16[4,128,768]{2,1,0:T(8,128)(2,1)} %fusion.126), calls=%async_computation | async-start | bytes 1572864 | tf_op jit(solution)/shard_map/while/body/eval_jaxpr/all_to_all | solution.py:70
  329.0 13.3 %collective-permute-start = (bf16[128,3072]{1,0:T(8,128)(2,1)S(1)}, bf16[128,3072]{1,0:T(8,128)(2,1)S(1)}, u32[]{:S(2)}, u32[]{:S(2)}) collective-permute-start(bf16[128,3072]{1,0:T(8,128)(2,1)S(1)} %broadcast_select_fusion.2), channel_id=1, source_target_pairs={{4,0},{8,4},{12,8},{16,12},{20,16},{24,20},{28,24},{5,1},{9,5},{13... | collective-permute-start | bytes 2359304 | tf_op jit(solution)/shard_map/while/body/eval_jaxpr/ppermute | solution.py:81
  342.3 10.4 %copy-start = (bf16[128,3072]{1,0:T(8,128)(2,1)}, bf16[128,3072]{1,0:T(8,128)(2,1)S(1)}, u32[]{:S(2)}) copy-start(bf16[128,3072]{1,0:T(8,128)(2,1)S(1)} %collective-permute-done) | copy-start | bytes 2359300 | tf_op jit(solution)/shard_map/while
  352.7 12.8 %all-to-all-start = ((bf16[4,128,768]{2,1,0:T(8,128)(2,1)}), bf16[4,128,768]{2,1,0:T(8,128)(2,1)S(1)}, u32[]{:S(2)}, u32[]{:S(2)}) async-start(bf16[4,128,768]{2,1,0:T(8,128)(2,1)} %fusion.126), calls=%async_computation | async-start | bytes 1572864 | tf_op jit(solution)/shard_map/while/body/eval_jaxpr/all_to_all | solution.py:70
  376.1 13.3 %collective-permute-start = (bf16[128,3072]{1,0:T(8,128)(2,1)S(1)}, bf16[128,3072]{1,0:T(8,128)(2,1)S(1)}, u32[]{:S(2)}, u32[]{:S(2)}) collective-permute-start(bf16[128,3072]{1,0:T(8,128)(2,1)S(1)} %broadcast_select_fusion.2), channel_id=1, source_target_pairs={{4,0},{8,4},{12,8},{16,12},{20,16},{24,20},{28,24},{5,1},{9,5},{13... | collective-permute-start | bytes 2359304 | tf_op jit(solution)/shard_map/while/body/eval_jaxpr/ppermute | solution.py:81
  389.4 10.4 %copy-start = (bf16[128,3072]{1,0:T(8,128)(2,1)}, bf16[128,3072]{1,0:T(8,128)(2,1)S(1)}, u32[]{:S(2)}) copy-start(bf16[128,3072]{1,0:T(8,128)(2,1)S(1)} %collective-permute-done) | copy-start | bytes 2359300 | tf_op jit(solution)/shard_map/while
  399.8 12.7 %all-to-all-start = ((bf16[4,128,768]{2,1,0:T(8,128)(2,1)}), bf16[4,128,768]{2,1,0:T(8,128)(2,1)S(1)}, u32[]{:S(2)}, u32[]{:S(2)}) async-start(bf16[4,128,768]{2,1,0:T(8,128)(2,1)} %fusion.126), calls=%async_computation | async-start | bytes 1572864 | tf_op jit(solution)/shard_map/while/body/eval_jaxpr/all_to_all | solution.py:70
  423.1 13.3 %collective-permute-start = (bf16[128,3072]{1,0:T(8,128)(2,1)S(1)}, bf16[128,3072]{1,0:T(8,128)(2,1)S(1)}, u32[]{:S(2)}, u32[]{:S(2)}) collective-permute-start(bf16[128,3072]{1,0:T(8,128)(2,1)S(1)} %broadcast_select_fusion.2), channel_id=1, source_target_pairs={{4,0},{8,4},{12,8},{16,12},{20,16},{24,20},{28,24},{5,1},{9,5},{13... | collective-permute-start | bytes 2359304 | tf_op jit(solution)/shard_map/while/body/eval_jaxpr/ppermute | solution.py:81
  436.4 10.4 %copy-start = (bf16[128,3072]{1,0:T(8,128)(2,1)}, bf16[128,3072]{1,0:T(8,128)(2,1)S(1)}, u32[]{:S(2)}) copy-start(bf16[128,3072]{1,0:T(8,128)(2,1)S(1)} %collective-permute-done) | copy-start | bytes 2359300 | tf_op jit(solution)/shard_map/while
  446.8 12.7 %all-to-all-start = ((bf16[4,128,768]{2,1,0:T(8,128)(2,1)}), bf16[4,128,768]{2,1,0:T(8,128)(2,1)S(1)}, u32[]{:S(2)}, u32[]{:S(2)}) async-start(bf16[4,128,768]{2,1,0:T(8,128)(2,1)} %fusion.126), calls=%async_computation | async-start | bytes 1572864 | tf_op jit(solution)/shard_map/while/body/eval_jaxpr/all_to_all | solution.py:70
  470.1 13.3 %collective-permute-start = (bf16[128,3072]{1,0:T(8,128)(2,1)S(1)}, bf16[128,3072]{1,0:T(8,128)(2,1)S(1)}, u32[]{:S(2)}, u32[]{:S(2)}) collective-permute-start(bf16[128,3072]{1,0:T(8,128)(2,1)S(1)} %broadcast_select_fusion.2), channel_id=1, source_target_pairs={{4,0},{8,4},{12,8},{16,12},{20,16},{24,20},{28,24},{5,1},{9,5},{13... | collective-permute-start | bytes 2359304 | tf_op jit(solution)/shard_map/while/body/eval_jaxpr/ppermute | solution.py:81
  483.4 10.4 %copy-start = (bf16[128,3072]{1,0:T(8,128)(2,1)}, bf16[128,3072]{1,0:T(8,128)(2,1)S(1)}, u32[]{:S(2)}) copy-start(bf16[128,3072]{1,0:T(8,128)(2,1)S(1)} %collective-permute-done) | copy-start | bytes 2359300 | tf_op jit(solution)/shard_map/while
  493.8 12.8 %all-to-all-start = ((bf16[4,128,768]{2,1,0:T(8,128)(2,1)}), bf16[4,128,768]{2,1,0:T(8,128)(2,1)S(1)}, u32[]{:S(2)}, u32[]{:S(2)}) async-start(bf16[4,128,768]{2,1,0:T(8,128)(2,1)} %fusion.126), calls=%async_computation | async-start | bytes 1572864 | tf_op jit(solution)/shard_map/while/body/eval_jaxpr/all_to_all | solution.py:70
  517.1 13.3 %collective-permute-start = (bf16[128,3072]{1,0:T(8,128)(2,1)S(1)}, bf16[128,3072]{1,0:T(8,128)(2,1)S(1)}, u32[]{:S(2)}, u32[]{:S(2)}) collective-permute-start(bf16[128,3072]{1,0:T(8,128)(2,1)S(1)} %broadcast_select_fusion.2), channel_id=1, source_target_pairs={{4,0},{8,4},{12,8},{16,12},{20,16},{24,20},{28,24},{5,1},{9,5},{13... | collective-permute-start | bytes 2359304 | tf_op jit(solution)/shard_map/while/body/eval_jaxpr/ppermute | solution.py:81
  530.5 10.4 %copy-start = (bf16[128,3072]{1,0:T(8,128)(2,1)}, bf16[128,3072]{1,0:T(8,128)(2,1)S(1)}, u32[]{:S(2)}) copy-start(bf16[128,3072]{1,0:T(8,128)(2,1)S(1)} %collective-permute-done) | copy-start | bytes 2359300 | tf_op jit(solution)/shard_map/while
  540.8 12.7 %all-to-all-start = ((bf16[4,128,768]{2,1,0:T(8,128)(2,1)}), bf16[4,128,768]{2,1,0:T(8,128)(2,1)S(1)}, u32[]{:S(2)}, u32[]{:S(2)}) async-start(bf16[4,128,768]{2,1,0:T(8,128)(2,1)} %fusion.126), calls=%async_computation | async-start | bytes 1572864 | tf_op jit(solution)/shard_map/while/body/eval_jaxpr/all_to_all | solution.py:70
  564.1 13.3 %collective-permute-start = (bf16[128,3072]{1,0:T(8,128)(2,1)S(1)}, bf16[128,3072]{1,0:T(8,128)(2,1)S(1)}, u32[]{:S(2)}, u32[]{:S(2)}) collective-permute-start(bf16[128,3072]{1,0:T(8,128)(2,1)S(1)} %broadcast_select_fusion.2), channel_id=1, source_target_pairs={{4,0},{8,4},{12,8},{16,12},{20,16},{24,20},{28,24},{5,1},{9,5},{13... | collective-permute-start | bytes 2359304 | tf_op jit(solution)/shard_map/while/body/eval_jaxpr/ppermute | solution.py:81
  577.4 10.4 %copy-start = (bf16[128,3072]{1,0:T(8,128)(2,1)}, bf16[128,3072]{1,0:T(8,128)(2,1)S(1)}, u32[]{:S(2)}) copy-start(bf16[128,3072]{1,0:T(8,128)(2,1)S(1)} %collective-permute-done) | copy-start | bytes 2359300 | tf_op jit(solution)/shard_map/while
  587.8 12.7 %all-to-all-start = ((bf16[4,128,768]{2,1,0:T(8,128)(2,1)}), bf16[4,128,768]{2,1,0:T(8,128)(2,1)S(1)}, u32[]{:S(2)}, u32[]{:S(2)}) async-start(bf16[4,128,768]{2,1,0:T(8,128)(2,1)} %fusion.126), calls=%async_computation | async-start | bytes 1572864 | tf_op jit(solution)/shard_map/while/body/eval_jaxpr/all_to_all | solution.py:70
  611.1 13.3 %collective-permute-start = (bf16[128,3072]{1,0:T(8,128)(2,1)S(1)}, bf16[128,3072]{1,0:T(8,128)(2,1)S(1)}, u32[]{:S(2)}, u32[]{:S(2)}) collective-permute-start(bf16[128,3072]{1,0:T(8,128)(2,1)S(1)} %broadcast_select_fusion.2), channel_id=1, source_target_pairs={{4,0},{8,4},{12,8},{16,12},{20,16},{24,20},{28,24},{5,1},{9,5},{13... | collective-permute-start | bytes 2359304 | tf_op jit(solution)/shard_map/while/body/eval_jaxpr/ppermute | solution.py:81
  624.4 10.4 %copy-start = (bf16[128,3072]{1,0:T(8,128)(2,1)}, bf16[128,3072]{1,0:T(8,128)(2,1)S(1)}, u32[]{:S(2)}) copy-start(bf16[128,3072]{1,0:T(8,128)(2,1)S(1)} %collective-permute-done) | copy-start | bytes 2359300 | tf_op jit(solution)/shard_map/while
  634.8 12.7 %all-to-all-start = ((bf16[4,128,768]{2,1,0:T(8,128)(2,1)}), bf16[4,128,768]{2,1,0:T(8,128)(2,1)S(1)}, u32[]{:S(2)}, u32[]{:S(2)}) async-start(bf16[4,128,768]{2,1,0:T(8,128)(2,1)} %fusion.126), calls=%async_computation | async-start | bytes 1572864 | tf_op jit(solution)/shard_map/while/body/eval_jaxpr/all_to_all | solution.py:70
  658.1 13.3 %collective-permute-start = (bf16[128,3072]{1,0:T(8,128)(2,1)S(1)}, bf16[128,3072]{1,0:T(8,128)(2,1)S(1)}, u32[]{:S(2)}, u32[]{:S(2)}) collective-permute-start(bf16[128,3072]{1,0:T(8,128)(2,1)S(1)} %broadcast_select_fusion.2), channel_id=1, source_target_pairs={{4,0},{8,4},{12,8},{16,12},{20,16},{24,20},{28,24},{5,1},{9,5},{13... | collective-permute-start | bytes 2359304 | tf_op jit(solution)/shard_map/while/body/eval_jaxpr/ppermute | solution.py:81
  671.4 10.4 %copy-start = (bf16[128,3072]{1,0:T(8,128)(2,1)}, bf16[128,3072]{1,0:T(8,128)(2,1)S(1)}, u32[]{:S(2)}) copy-start(bf16[128,3072]{1,0:T(8,128)(2,1)S(1)} %collective-permute-done) | copy-start | bytes 2359300 | tf_op jit(solution)/shard_map/while
  681.8 12.7 %all-to-all-start = ((bf16[4,128,768]{2,1,0:T(8,128)(2,1)}), bf16[4,128,768]{2,1,0:T(8,128)(2,1)S(1)}, u32[]{:S(2)}, u32[]{:S(2)}) async-start(bf16[4,128,768]{2,1,0:T(8,128)(2,1)} %fusion.126), calls=%async_computation | async-start | bytes 1572864 | tf_op jit(solution)/shard_map/while/body/eval_jaxpr/all_to_all | solution.py:70
  705.1 13.3 %collective-permute-start = (bf16[128,3072]{1,0:T(8,128)(2,1)S(1)}, bf16[128,3072]{1,0:T(8,128)(2,1)S(1)}, u32[]{:S(2)}, u32[]{:S(2)}) collective-permute-start(bf16[128,3072]{1,0:T(8,128)(2,1)S(1)} %broadcast_select_fusion.2), channel_id=1, source_target_pairs={{4,0},{8,4},{12,8},{16,12},{20,16},{24,20},{28,24},{5,1},{9,5},{13... | collective-permute-start | bytes 2359304 | tf_op jit(solution)/shard_map/while/body/eval_jaxpr/ppermute | solution.py:81
  718.4 10.4 %copy-start = (bf16[128,3072]{1,0:T(8,128)(2,1)}, bf16[128,3072]{1,0:T(8,128)(2,1)S(1)}, u32[]{:S(2)}) copy-start(bf16[128,3072]{1,0:T(8,128)(2,1)S(1)} %collective-permute-done) | copy-start | bytes 2359300 | tf_op jit(solution)/shard_map/while
  728.8 12.7 %all-to-all-start = ((bf16[4,128,768]{2,1,0:T(8,128)(2,1)}), bf16[4,128,768]{2,1,0:T(8,128)(2,1)S(1)}, u32[]{:S(2)}, u32[]{:S(2)}) async-start(bf16[4,128,768]{2,1,0:T(8,128)(2,1)} %fusion.126), calls=%async_computation | async-start | bytes 1572864 | tf_op jit(solution)/shard_map/while/body/eval_jaxpr/all_to_all | solution.py:70
  752.1 13.3 %collective-permute-start = (bf16[128,3072]{1,0:T(8,128)(2,1)S(1)}, bf16[128,3072]{1,0:T(8,128)(2,1)S(1)}, u32[]{:S(2)}, u32[]{:S(2)}) collective-permute-start(bf16[128,3072]{1,0:T(8,128)(2,1)S(1)} %broadcast_select_fusion.2), channel_id=1, source_target_pairs={{4,0},{8,4},{12,8},{16,12},{20,16},{24,20},{28,24},{5,1},{9,5},{13... | collective-permute-start | bytes 2359304 | tf_op jit(solution)/shard_map/while/body/eval_jaxpr/ppermute | solution.py:81
  765.4 10.4 %copy-start = (bf16[128,3072]{1,0:T(8,128)(2,1)}, bf16[128,3072]{1,0:T(8,128)(2,1)S(1)}, u32[]{:S(2)}) copy-start(bf16[128,3072]{1,0:T(8,128)(2,1)S(1)} %collective-permute-done) | copy-start | bytes 2359300 | tf_op jit(solution)/shard_map/while
  775.8 12.7 %all-to-all-start = ((bf16[4,128,768]{2,1,0:T(8,128)(2,1)}), bf16[4,128,768]{2,1,0:T(8,128)(2,1)S(1)}, u32[]{:S(2)}, u32[]{:S(2)}) async-start(bf16[4,128,768]{2,1,0:T(8,128)(2,1)} %fusion.126), calls=%async_computation | async-start | bytes 1572864 | tf_op jit(solution)/shard_map/while/body/eval_jaxpr/all_to_all | solution.py:70
  799.1 13.3 %collective-permute-start = (bf16[128,3072]{1,0:T(8,128)(2,1)S(1)}, bf16[128,3072]{1,0:T(8,128)(2,1)S(1)}, u32[]{:S(2)}, u32[]{:S(2)}) collective-permute-start(bf16[128,3072]{1,0:T(8,128)(2,1)S(1)} %broadcast_select_fusion.2), channel_id=1, source_target_pairs={{4,0},{8,4},{12,8},{16,12},{20,16},{24,20},{28,24},{5,1},{9,5},{13... | collective-permute-start | bytes 2359304 | tf_op jit(solution)/shard_map/while/body/eval_jaxpr/ppermute | solution.py:81
  812.4 10.4 %copy-start = (bf16[128,3072]{1,0:T(8,128)(2,1)}, bf16[128,3072]{1,0:T(8,128)(2,1)S(1)}, u32[]{:S(2)}) copy-start(bf16[128,3072]{1,0:T(8,128)(2,1)S(1)} %collective-permute-done) | copy-start | bytes 2359300 | tf_op jit(solution)/shard_map/while
  822.8 12.7 %all-to-all-start = ((bf16[4,128,768]{2,1,0:T(8,128)(2,1)}), bf16[4,128,768]{2,1,0:T(8,128)(2,1)S(1)}, u32[]{:S(2)}, u32[]{:S(2)}) async-start(bf16[4,128,768]{2,1,0:T(8,128)(2,1)} %fusion.126), calls=%async_computation | async-start | bytes 1572864 | tf_op jit(solution)/shard_map/while/body/eval_jaxpr/all_to_all | solution.py:70
  846.0 12.2 %slice-start = ((s8[6291456]{0:T(1024)(128)(4,1)}), s8[2097152]{0:T(1024)(128)(4,1)S(1)}, s32[]{:S(2)}) async-start(s8[6291456]{0:T(1024)(128)(4,1)} %bitcast.149), calls=%async_computation.2 | async-start | bytes 4194304
  846.0 75.8 %all-to-all-start.1 = ((bf16[4,1024,768]{1,2,0:T(8,128)(2,1)}), bf16[4,1024,768]{1,2,0:T(8,128)(2,1)}, u32[]{:S(2)}, u32[]{:S(2)}) async-start(bf16[4,1024,768]{1,2,0:T(8,128)(2,1)} %convert_bitcast_fusion.1), calls=%async_computation.1 | async-start | bytes 12582912 | tf_op jit(solution)/shard_map/all_to_all | solution.py:70
  851.4 116.4 %collective-permute-start.1 = (bf16[8,128,3072]{2,1,0:T(8,128)(2,1)}, bf16[8,128,3072]{2,1,0:T(8,128)(2,1)}, u32[]{:S(2)}, u32[]{:S(2)}) collective-permute-start(bf16[8,128,3072]{2,1,0:T(8,128)(2,1)} %get-tuple-element.242), channel_id=1, source_target_pairs={{4,0},{8,4},{12,8},{16,12},{20,16},{24,20},{28,24},{5,1},{9,5},{13... | collective-permute-start | bytes 18874376 | tf_op jit(solution)/shard_map/ppermute | solution.py:144
  853.3 4.9 slice-start.1
  858.2 8.3 copy-start.3
  858.2 8.3 copy-start.5
  971.3 2.8 copy-start.2

commit v2 on v1

v2 whole, which is shorter than its diff:
```python
import functools

import jax
import jax.numpy as jnp
from jax import lax
from jax.experimental import pallas as pl
from jax.experimental.pallas import tpu as pltpu
from jax.sharding import PartitionSpec as P

gelu_scale = 0.7978845608028654
gelu_cubic = 0.044715
LANES = 128
ROWS = 64
MESH = pl.DeviceIdType.MESH


def gelu_both(values):
    square = values * values
    tangent = jnp.tanh(gelu_scale * (values + gelu_cubic * square * values))
    value = 0.5 * values * (1.0 + tangent)
    slope = 0.5 * (1.0 + tangent) + 0.5 * values * (1.0 - tangent * tangent) * gelu_scale * (
        1.0 + 3.0 * gelu_cubic * square
    )
    return value, slope


def running_rank(member):
    rows, width = member.shape
    tile = LANES
    pieces = member.reshape(rows, width // tile, tile).astype(jnp.bfloat16)
    upper = jnp.triu(jnp.ones((tile, tile), jnp.bfloat16))
    inner = jnp.einsum("rbi,ij->rbj", pieces, upper, preferred_element_type=jnp.float32)
    totals = inner[:, :, -1].astype(jnp.bfloat16)
    blocks = width // tile
    strict = jnp.triu(jnp.ones((blocks, blocks), jnp.bfloat16), 1)
    before = jnp.einsum("rb,bc->rc", totals, strict, preferred_element_type=jnp.float32)
    return (inner + before[:, :, None]).reshape(rows, width).astype(jnp.int32) - 1


def mixing(source_row, group_index, group_count):
    feat_count = source_row.shape[0] // group_count
    per_peer = feat_count // group_count
    slots = -(-per_peer // LANES) * LANES
    targets = source_row.reshape(group_count, feat_count)
    groups = targets // feat_count
    place = jnp.arange(slots, dtype=jnp.int32)

    mine = groups == group_index
    rank = jnp.where(mine, running_rank(mine), -1)
    feature = targets - group_index * feat_count
    hit = rank[:, None, :] == place[None, :, None]
    chosen = jnp.sum(jnp.where(hit, feature[:, None, :] + 1, 0), axis=2) - 1

    own = lax.dynamic_index_in_dim(groups, group_index, 0, keepdims=False)
    sources = jnp.arange(group_count, dtype=jnp.int32)[:, None]
    member = own[None, :] == sources
    landing = jnp.sum(jnp.where(member, running_rank(member) + sources * slots, 0), axis=0)
    return chosen.reshape(-1), landing, slots


def dot(left, right, left_dim=1, right_dim=0):
    return lax.dot_general(
        left, right, (((left_dim,), (right_dim,)), ((), ())), preferred_element_type=jnp.float32
    )


def relay_kernel(
    sections, groups, slots,
    inputs, last_grads, first, first_turned, second_turned, chosen, landing,
    grads_out, befores_out, cotangents_out, came_out, sent_out, slopes_out,
    leaving, back_mix, cotangents, arrived, slopes, grads, befores, sending,
    in_sem, slope_sem, grad_sem, before_sem, sent_sem, keep_sem,
    send_sem, recv_sem, relay_send, relay_recv, swap_send, swap_recv, swap_own,
):
    section = lax.axis_index("pipe")
    group = lax.axis_index("tensor")
    last = sections - 1
    chunks, rows, feats = inputs.shape
    size = first.shape[1]
    depth = arrived.shape[0]
    tile = 512 if feats % 512 == 0 else 256

    def peer(offset):
        return lax.rem(group + offset, groups)

    def source(offset):
        return lax.rem(group + (groups - offset), groups)

    barrier = pltpu.get_barrier_semaphore()
    for offset in range(1, groups):
        pl.semaphore_signal(barrier, inc=1, device_id={"tensor": peer(offset)}, device_id_type=MESH)

    for beside in (lax.rem(section + 1, sections), lax.rem(section + last, sections)):
        pl.semaphore_signal(barrier, inc=1, device_id={"pipe": beside}, device_id_type=MESH)
    pl.semaphore_wait(barrier, groups + 1)

    def load_last(chunk):
        return pltpu.make_async_copy(
            last_grads.at[chunk], cotangents.at[chunk], relay_recv.at[chunk]
        )

    @pl.when(section == last)
    def _():
        lax.fori_loop(0, chunks, lambda m, _: (load_last(m).start(), 0)[1], 0)

    def load_input(chunk, slot):
        return pltpu.make_async_copy(inputs.at[chunk], grads.at[slot], in_sem.at[slot])

    load_input(0, 0).start()

    step = 256

    def build_leaving(index, _):
        at = pl.ds(pl.multiple_of(index * LANES, LANES), LANES)
        column = chosen[at, :]
        for left in range(0, feats, step):
            lane = lax.broadcasted_iota(jnp.int32, (LANES, step), 1) + left
            leaving[at, left : left + step] = jnp.where(column == lane, 1.0, 0.0).astype(jnp.bfloat16)
        return 0

    lax.fori_loop(0, groups * slots // LANES, build_leaving, 0)

    def build_back(block, _):
        at = pl.ds(pl.multiple_of(block * size, size), size)
        column = landing[at, :]
        turned = second_turned[block]
        for peer_index in range(groups):
            for left in range(0, slots, LANES):
                lane = lax.broadcasted_iota(jnp.int32, (size, LANES), 1) + (peer_index * slots + left)
                spread = jnp.where(column == lane, 1.0, 0.0).astype(jnp.bfloat16)
                back_mix[peer_index, at, left : left + LANES] = dot(turned, spread).astype(jnp.bfloat16)
        return 0

    lax.fori_loop(0, feats // size, build_back, 0)

    def store_slope(chunk, slot):
        return pltpu.make_async_copy(befores.at[slot], slopes_out.at[chunk], before_sem.at[slot])

    def store_sent(chunk, slot):
        return pltpu.make_async_copy(sending.at[slot], sent_out.at[:, chunk], sent_sem.at[slot])

    def forward(chunk, _):
        slot = lax.rem(chunk, 2)
        load_input(chunk, slot).wait()

        @pl.when(chunk + 1 < chunks)
        def _():
            load_input(chunk + 1, 1 - slot).start()

        @pl.when(chunk >= 2)
        def _():
            store_slope(chunk - 2, slot).wait()
            store_sent(chunk - 2, slot).wait()

        def one_block(block, _):
            at = pl.ds(pl.multiple_of(block * size, size), size)
            value, slope = gelu_both(dot(grads[slot, :, at], first[block]))
            slopes[0, :, at] = value.astype(jnp.bfloat16)
            befores[slot, :, at] = slope.astype(jnp.bfloat16)
            return 0

        lax.fori_loop(0, feats // size, one_block, 0, unroll=2)
        for target in range(groups):
            sending[slot, target] = dot(
                slopes[0], leaving[target * slots : (target + 1) * slots, :], 1, 1
            ).astype(jnp.bfloat16)
        store_slope(chunk, slot).start()
        store_sent(chunk, slot).start()
        return 0

    lax.fori_loop(0, chunks, forward, 0)
    for chunk in range(chunks - 2, chunks):
        store_slope(chunk, chunk % 2).wait()
        store_sent(chunk, chunk % 2).wait()

    def swap(offset):
        return pltpu.make_async_remote_copy(
            src_ref=sent_out.at[peer(offset)],
            dst_ref=came_out.at[group],
            send_sem=swap_send.at[offset],
            recv_sem=swap_recv.at[offset],
            device_id={"tensor": peer(offset)},
            device_id_type=MESH,
        )

    own_swap = pltpu.make_async_copy(sent_out.at[group], came_out.at[group], swap_own)

    def start_swap():
        for offset in range(1, groups):
            swap(offset).start()
        own_swap.start()

    @pl.when(section * 2 < sections)
    def _():
        start_swap()

    def mix_copy(chunk, slot, offset):
        target = peer(offset)
        return pltpu.make_async_remote_copy(
            src_ref=sending.at[slot, target],
            dst_ref=arrived.at[lax.rem(chunk, depth), group],
            send_sem=send_sem.at[slot, offset],
            recv_sem=recv_sem.at[chunk, offset],
            device_id={"tensor": target},
            device_id_type=MESH,
        )

    def mix_wait(chunk, slot, offset):
        origin = source(offset)
        pltpu.make_async_remote_copy(
            src_ref=sending.at[slot, origin],
            dst_ref=arrived.at[lax.rem(chunk, depth), origin],
            send_sem=send_sem.at[slot, offset],
            recv_sem=recv_sem.at[chunk, offset],
            device_id={"tensor": origin},
            device_id_type=MESH,
        ).wait_recv()

    def relay_copy(chunk, slot, target):
        return pltpu.make_async_remote_copy(
            src_ref=grads.at[slot],
            dst_ref=cotangents.at[chunk],
            send_sem=relay_send.at[slot],
            recv_sem=relay_recv.at[chunk],
            device_id={"pipe": target},
            device_id_type=MESH,
        )

    def load_slope(chunk, slot):
        return pltpu.make_async_copy(slopes_out.at[chunk], slopes.at[slot], slope_sem.at[slot])

    def store_cotangent(chunk):
        return pltpu.make_async_copy(
            cotangents.at[chunk], cotangents_out.at[chunk], keep_sem.at[chunk]
        )

    def store_grad(chunk, slot):
        return pltpu.make_async_copy(grads.at[slot], grads_out.at[chunk], grad_sem.at[slot])

    def store_before(chunk, slot):
        return pltpu.make_async_copy(befores.at[slot], befores_out.at[chunk], before_sem.at[slot])

    def first_half(chunk, slot):
        @pl.when(section == last)
        def _():
            load_last(chunk).wait()

        @pl.when(section < last)
        def _():
            relay_copy(chunk, slot, section + 1).wait_recv()

        load_slope(chunk, slot).start()
        store_cotangent(chunk).start()
        for offset in range(1, groups):
            target = peer(offset)
            sending[slot, target] = dot(cotangents[chunk], back_mix[target]).astype(jnp.bfloat16)
            mix_copy(chunk, slot, offset).start()
        arrived[lax.rem(chunk, depth), group] = dot(cotangents[chunk], back_mix[group]).astype(
            jnp.bfloat16
        )

    def leave(chunk, slot):
        store_grad(chunk, slot).wait()
        store_before(chunk, slot).wait()

        @pl.when(section > 0)
        def _():
            relay_copy(chunk, slot, section - 1).wait_send()

    def second_half(chunk, slot):
        for offset in range(1, groups):
            mix_wait(chunk, slot, offset)
        load_slope(chunk, slot).wait()

        @pl.when(chunk >= 2)
        def _():
            leave(chunk - 2, slot)

        held = lax.rem(chunk, depth)

        def one_tile(index, _):
            start = pl.multiple_of(index * tile, tile)
            at = pl.ds(start, tile)
            total = dot(arrived[held, 0], leaving[0:slots, at])
            for origin in range(1, groups):
                total += dot(
                    arrived[held, origin], leaving[origin * slots : (origin + 1) * slots, at]
                )
            before = (total * slopes[slot, :, at].astype(jnp.float32)).astype(jnp.bfloat16)
            befores[slot, :, at] = before
            for piece in range(tile // size):
                here = pl.ds(pl.multiple_of(start + piece * size, size), size)
                back = dot(
                    before[:, piece * size : (piece + 1) * size],
                    first_turned[index * (tile // size) + piece],
                )
                grads[slot, :, here] = (
                    cotangents[chunk, :, here].astype(jnp.float32) + back
                ).astype(jnp.bfloat16)
            return 0

        lax.fori_loop(0, feats // tile, one_tile, 0)

        @pl.when(section > 0)
        def _():
            relay_copy(chunk, slot, section - 1).start()

        store_grad(chunk, slot).start()
        store_before(chunk, slot).start()
        for offset in range(1, groups):
            mix_copy(chunk, slot, offset).wait_send()

    first_half(0, 0)

    def advance(chunk, _):
        slot = lax.rem(chunk, 2)

        @pl.when(chunk + 1 < chunks)
        def _():
            first_half(chunk + 1, 1 - slot)

        second_half(chunk, slot)
        return 0

    lax.fori_loop(0, chunks, advance, 0)

    @pl.when(section * 2 >= sections)
    def _():
        start_swap()

    for chunk in range(chunks - 2, chunks):
        leave(chunk, chunk % 2)
    lax.fori_loop(0, chunks, lambda m, _: (store_cotangent(m).wait(), 0)[1], 0)
    for offset in range(1, groups):
        swap(offset).wait()
    own_swap.wait()


def weight_kernel(came, landing, kept, cotangents, inputs, befores, first_out, second_out):
    groups, tokens, slots = came.shape
    count, size, _ = first_out.shape
    where = landing[...]
    mixed = jnp.zeros((tokens, where.shape[1]), jnp.float32)
    for origin in range(groups):
        slot = lax.broadcasted_iota(jnp.int32, (slots, where.shape[1]), 0) + origin * slots
        spread = jnp.where(slot == where, 1.0, 0.0).astype(jnp.bfloat16)
        mixed += dot(came[origin], spread)
    mixed = mixed.astype(jnp.bfloat16)
    for piece in range(count):
        at = slice(piece * size, (piece + 1) * size)
        second_out[piece] = dot(mixed[:, at], cotangents[:, at], 0, 0) * kept[0, 0]
        first_out[piece] = dot(inputs[:, at], befores[:, at], 0, 0)


def on_device(section_inputs, out_grad, w_first, w_second, drop_flags, perm):
    sections = lax.axis_size("pipe")
    groups = lax.axis_size("tensor")
    _, micro_count, token_count, feats = section_inputs.shape
    tokens = micro_count * token_count
    first = w_first[0, 0]
    blocks, size, _ = first.shape
    kept = drop_flags[0, 0]
    chosen, landing, slots = mixing(perm[0, 0], lax.axis_index("tensor"), groups)
    rows = ROWS
    chunks = tokens // rows
    depth = min(4, chunks)
    chunked = (chunks, rows, feats)

    def made(*shape):
        return jax.ShapeDtypeStruct(shape, jnp.bfloat16)

    def room(*shape):
        return pltpu.VMEM(shape, jnp.bfloat16)

    sem = pltpu.SemaphoreType.DMA
    anywhere = pl.BlockSpec(memory_space=pl.ANY)
    vmem = pl.BlockSpec(memory_space=pltpu.VMEM)
    swapped = (groups, chunks, rows, slots)
    grads, befores, cotangents, came, _, _ = pl.pallas_call(
        functools.partial(relay_kernel, sections, groups, slots),
        out_shape=[made(*chunked)] * 3 + [made(*swapped)] * 2 + [made(*chunked)],
        in_specs=[anywhere] * 2 + [vmem] * 5,
        out_specs=[anywhere] * 6,
        scratch_shapes=[
            room(groups * slots, feats),
            room(groups, feats, slots),
            room(*chunked),
            room(depth, groups, rows, slots),
            room(2, rows, feats),
            room(2, rows, feats),
            room(2, rows, feats),
            room(2, groups, rows, slots),
            sem((2,)), sem((2,)), sem((2,)), sem((2,)), sem((2,)), sem((chunks,)),
            sem((2, groups)), sem((chunks, groups)), sem((2,)), sem((chunks,)),
            sem((groups,)), sem((groups,)), sem(()),
        ],
        compiler_params=pltpu.CompilerParams(
            collective_id=0, has_side_effects=True, vmem_limit_bytes=62 * 2**20
        ),
    )(
        section_inputs.reshape(chunked),
        out_grad.reshape(chunked),
        first,
        jnp.swapaxes(first, 1, 2),
        jnp.swapaxes(w_second[0, 0], 1, 2) * kept.astype(jnp.bfloat16),
        chosen[:, None],
        landing[:, None],
    )

    wide = 256
    tall = pl.BlockSpec((tokens, wide), lambda i: (0, i))
    out = pl.BlockSpec((wide // size, size, size), lambda i: (i, 0, 0))
    weights = jax.ShapeDtypeStruct((blocks, size, size), jnp.float32)
    first_grad, second_grad = pl.pallas_call(
        weight_kernel,
        grid=(feats // wide,),
        out_shape=[weights] * 2,
        in_specs=[
            pl.BlockSpec((groups, tokens, slots), lambda i: (0, 0, 0)),
            pl.BlockSpec((1, wide), lambda i: (0, i)),
            pl.BlockSpec(memory_space=pltpu.SMEM),
            tall, tall, tall,
        ],
        out_specs=[out] * 2,
        compiler_params=pltpu.CompilerParams(vmem_limit_bytes=56 * 2**20),
    )(
        came.reshape(groups, tokens, slots),
        landing[None, :],
        kept.astype(jnp.float32).reshape(1, 1),
        cotangents.reshape(tokens, feats),
        section_inputs.reshape(tokens, feats),
        befores.reshape(tokens, feats),
    )
    return grads.reshape(section_inputs.shape), first_grad[None, None], second_grad[None, None]


def solution(mesh):
    placed = (
        P("pipe", None, None, "tensor"),
        P(None, None, "tensor"),
        P("pipe", None, "tensor", None, None),
        P("pipe", None, "tensor", None, None),
        P("pipe", None),
        P("pipe", None, None),
    )
    return jax.shard_map(
        on_device,
        mesh=mesh,
        in_specs=placed,
        out_specs=(
            P("pipe", None, None, "tensor"),
            P("pipe", None, "tensor", None, None),
            P("pipe", None, "tensor", None, None),
        ),
        check_vma=False,
    )
```

time: 992 us -> 529 us (0.53)
  the two profiles are of different devices: /device:TPU:17 before, /device:TPU:0 now
where the time goes in v2:
time: 529 us; the launch traced here: 528 us
  Pallas kernels  506 us (96%)
  local copies, waits for them, and re-layouts  10.8 us (2%)
  other arithmetic  9 us (2%)
    pallas_call x1, Pallas kernels, on_device(): pl.pallas_call(functools.partial(relay_kernel, sections, groups, slots),...  470 us
    pallas_call x1, Pallas kernels, on_device(): pl.pallas_call(weight_kernel, grid=(feats // wide,), out_shape=[weights]...  36.7 us

profile of v2, /device:TPU:0, one launch (start us, length us, event | category | flops | bytes accessed | tf_op | source)
XLA Modules:
  0.0 528.3 jit_solution(14459666405589799726)
XLA Ops:
  1.3 1.1 and_reduce_fusion
  2.5 0.5 broadcast.166
  3.0 1.8 fusion.37
  4.8 0.2 fusion.3
  5.0 0.2 fusion.10
  5.2 0.1 fusion.22
  5.3 0.1 add_bitcast_fusion
  5.5 0.2 fusion.2
  5.7 0.2 fusion.11
  5.8 0.1 fusion.20
  6.0 0.1 select_reduce_fusion.1
  6.1 0.0 copy-start.1
  6.1 4.9 select_reduce_fusion
  11.0 1.5 copy.18
  12.5 1.0 multiply_bitcast_fusion.second_turned
  13.5 2.3 copy.17
  15.8 1.7 copy.25
  17.4 1.7 copy.21.landing
  19.1 469.8 %shard_map.85 = (bf16[16,64,3072]{2,1,0:T(8,128)(2,1)}, bf16[16,64,3072]{2,1,0:T(8,128)(2,1)}, bf16[16,64,3072]{2,1,0:T(8,128)(2,1)}, bf16[4,16,64,768]{3,2,1,0:...) custom-call(bf16[16,64,3072]{2,1,0:T(8,128)(2,1)} %bitcast.38, ...), custom_call_target="tpu_custom_call" | custom-call | tf_op jit(solution)/shard_map/pallas_call | solution.py:379
  488.9 0.0 copy-done.1
  488.9 0.0 copy-start
  488.9 36.7 %shard_map.86 = (f32[24,128,128]{2,1,0:T(8,128)}, f32[24,128,128]{2,1,0:T(8,128)}) custom-call(bf16[4,1024,768]{2,1,0:T(8,128)(2,1)} %bitcast.45, s32[1,3072]{1,0:T(1,128)} %bitcast.49, f32[1,1]{1,0:T(1,128)S(6)} %convert_element_type.38.kept, bf16[1024,3072]{1,0:T(8,128)(2,1)} %bitcast.44, bf16[1024,3072]{1,0:T(8,128)(2,1)} %bitcast.39, ...), custom_call_target="tpu_custom_call" | custom-call | tf_op jit(solution)/shard_map/pallas_call | solution.py:414
  525.6 0.0 copy-done
  525.6 2.7 copy.29
  (9 shorter events, 0.1 us)
Async XLA Ops:
  6.1 482.8 %copy-start.1 = (s32[24,128]{1,0:T(8,128)}, s32[24,128]{1,0:T(8,128)S(1)}, u32[]{:S(2)}) copy-start(s32[24,128]{1,0:T(8,128)S(1)} %select_reduce_fusion.1) | copy-start | bytes 36868
  488.9 36.7 %copy-start = (bf16[16,64,3072]{2,1,0:T(8,128)(2,1)S(1)}, bf16[16,64,3072]{2,1,0:T(8,128)(2,1)}, u32[]{:S(2)}) copy-start(bf16[16,64,3072]{2,1,0:T(8,128)(2,1)} %get-tuple-element.9) | copy-start | bytes 18874372

commit v3 on v2

--- a/solution.py
+++ b/solution.py
@@ -10,7 +10,7 @@
 gelu_scale = 0.7978845608028654
 gelu_cubic = 0.044715
 LANES = 128
-ROWS = 64
+ROWS = 128
 MESH = pl.DeviceIdType.MESH
 
 
@@ -79,6 +79,9 @@
     size = first.shape[1]
     depth = arrived.shape[0]
     tile = 512 if feats % 512 == 0 else 256
+    parts = 3 if feats // tile % 3 == 0 else 1
+    part = feats // parts
+    late = section >= sections - 2
 
     def peer(offset):
         return lax.rem(group + offset, groups)
@@ -96,7 +99,7 @@
 
     def load_last(chunk):
         return pltpu.make_async_copy(
-            last_grads.at[chunk], cotangents.at[chunk], relay_recv.at[chunk]
+            last_grads.at[chunk], cotangents.at[chunk], relay_recv.at[chunk, 0]
         )
 
     @pl.when(section == last)
@@ -105,8 +108,6 @@
 
     def load_input(chunk, slot):
         return pltpu.make_async_copy(inputs.at[chunk], grads.at[slot], in_sem.at[slot])
-
-    load_input(0, 0).start()
 
     step = 256
 
@@ -139,7 +140,7 @@
     def store_sent(chunk, slot):
         return pltpu.make_async_copy(sending.at[slot], sent_out.at[:, chunk], sent_sem.at[slot])
 
-    def forward(chunk, _):
+    def forward(with_slope, with_value, chunk, _):
         slot = lax.rem(chunk, 2)
         load_input(chunk, slot).wait()
 
@@ -149,29 +150,47 @@
 
         @pl.when(chunk >= 2)
         def _():
-            store_slope(chunk - 2, slot).wait()
-            store_sent(chunk - 2, slot).wait()
+            done(with_slope, with_value, chunk - 2, slot)
 
         def one_block(block, _):
             at = pl.ds(pl.multiple_of(block * size, size), size)
             value, slope = gelu_both(dot(grads[slot, :, at], first[block]))
-            slopes[0, :, at] = value.astype(jnp.bfloat16)
-            befores[slot, :, at] = slope.astype(jnp.bfloat16)
+            if with_value:
+                slopes[0, :, at] = value.astype(jnp.bfloat16)
+            if with_slope:
+                befores[slot, :, at] = slope.astype(jnp.bfloat16)
             return 0
 
         lax.fori_loop(0, feats // size, one_block, 0, unroll=2)
-        for target in range(groups):
-            sending[slot, target] = dot(
-                slopes[0], leaving[target * slots : (target + 1) * slots, :], 1, 1
-            ).astype(jnp.bfloat16)
-        store_slope(chunk, slot).start()
-        store_sent(chunk, slot).start()
+        if with_value:
+            for target in range(groups):
+                sending[slot, target] = dot(
+                    slopes[0], leaving[target * slots : (target + 1) * slots, :], 1, 1
+                ).astype(jnp.bfloat16)
+            store_sent(chunk, slot).start()
+        if with_slope:
+            store_slope(chunk, slot).start()
         return 0
 
-    lax.fori_loop(0, chunks, forward, 0)
-    for chunk in range(chunks - 2, chunks):
-        store_slope(chunk, chunk % 2).wait()
-        store_sent(chunk, chunk % 2).wait()
+    def done(with_slope, with_value, chunk, slot):
+        if with_slope:
+            store_slope(chunk, slot).wait()
+        if with_value:
+            store_sent(chunk, slot).wait()
+
+    def recompute(with_slope, with_value):
+        load_input(0, 0).start()
+        lax.fori_loop(0, chunks, functools.partial(forward, with_slope, with_value), 0)
+        for chunk in range(chunks - 2, chunks):
+            done(with_slope, with_value, chunk, chunk % 2)
+
+    @pl.when(late)
+    def _():
+        recompute(True, False)
+
+    @pl.when(section < sections - 2)
+    def _():
+        recompute(True, True)
 
     def swap(offset):
         return pltpu.make_async_remote_copy(
@@ -216,12 +235,13 @@
             device_id_type=MESH,
         ).wait_recv()
 
-    def relay_copy(chunk, slot, target):
+    def relay_copy(chunk, slot, target, piece):
+        at = pl.ds(piece * part, part)
         return pltpu.make_async_remote_copy(
-            src_ref=grads.at[slot],
-            dst_ref=cotangents.at[chunk],
-            send_sem=relay_send.at[slot],
-            recv_sem=relay_recv.at[chunk],
+            src_ref=grads.at[slot, :, at],
+            dst_ref=cotangents.at[chunk, :, at],
+            send_sem=relay_send.at[slot, piece],
+            recv_sem=relay_recv.at[chunk, piece],
             device_id={"pipe": target},
             device_id_type=MESH,
         )
@@ -247,7 +267,8 @@
 
         @pl.when(section < last)
         def _():
-            relay_copy(chunk, slot, section + 1).wait_recv()
+            for piece in range(parts):
+                relay_copy(chunk, slot, section + 1, piece).wait_recv()
 
         load_slope(chunk, slot).start()
         store_cotangent(chunk).start()
@@ -265,7 +286,8 @@
 
         @pl.when(section > 0)
         def _():
-            relay_copy(chunk, slot, section - 1).wait_send()
+            for piece in range(parts):
+                relay_copy(chunk, slot, section - 1, piece).wait_send()
 
     def second_half(chunk, slot):
         for offset in range(1, groups):
@@ -299,11 +321,13 @@
                 ).astype(jnp.bfloat16)
             return 0
 
-        lax.fori_loop(0, feats // tile, one_tile, 0)
-
-        @pl.when(section > 0)
-        def _():
-            relay_copy(chunk, slot, section - 1).start()
+        each = feats // tile // parts
+        for piece in range(parts):
+            lax.fori_loop(piece * each, (piece + 1) * each, one_tile, 0)
+
+            @pl.when(section > 0)
+            def _():
+                relay_copy(chunk, slot, section - 1, piece).start()
 
         store_grad(chunk, slot).start()
         store_before(chunk, slot).start()
@@ -324,12 +348,17 @@
 
     lax.fori_loop(0, chunks, advance, 0)
 
-    @pl.when(section * 2 >= sections)
-    def _():
-        start_swap()
-
     for chunk in range(chunks - 2, chunks):
         leave(chunk, chunk % 2)
+
+    @pl.when(late)
+    def _():
+        recompute(False, True)
+
+    @pl.when(section * 2 >= sections)
+    def _():
+        start_swap()
+
     lax.fori_loop(0, chunks, lambda m, _: (store_cotangent(m).wait(), 0)[1], 0)
     for offset in range(1, groups):
         swap(offset).wait()
@@ -391,7 +420,7 @@
             room(2, rows, feats),
             room(2, groups, rows, slots),
             sem((2,)), sem((2,)), sem((2,)), sem((2,)), sem((2,)), sem((chunks,)),
-            sem((2, groups)), sem((chunks, groups)), sem((2,)), sem((chunks,)),
+            sem((2, groups)), sem((chunks, groups)), sem((2, 3)), sem((chunks, 3)),
             sem((groups,)), sem((groups,)), sem(()),
         ],
         compiler_params=pltpu.CompilerParams(

time: 529 us -> 353 us (0.67)
  Pallas kernels: 506 us -> 331 us
    pallas_call x1, Pallas kernels: 470 us -> 294 us  [on_device(): pl.pallas_call(functools.partial(relay_kernel, sections, groups, slots),...]
where the time goes in v3:
time: 353 us
  Pallas kernels  331 us (94%)
  local copies, waits for them, and re-layouts  10.8 us (3%)
  other arithmetic  9 us (3%)
    pallas_call x1, Pallas kernels, on_device(): pl.pallas_call(functools.partial(relay_kernel, sections, groups, slots),...  294 us
    pallas_call x1, Pallas kernels, on_device(): pl.pallas_call(weight_kernel, grid=(feats // wide,), out_shape=[weights]...  36.7 us
    unnamed x9, local copies, waits for them, and re-layouts  8.18 us

profile of v3, /device:TPU:0, one launch (start us, length us, event | category | flops | bytes accessed | tf_op | source)
XLA Modules:
  0.0 352.6 jit_solution(508226075043071211)
XLA Ops:
  1.3 1.1 and_reduce_fusion
  2.5 0.5 broadcast.166
  3.0 1.8 fusion.37
  4.8 0.2 fusion.3
  5.0 0.2 fusion.10
  5.2 0.1 fusion.22
  5.3 0.1 add_bitcast_fusion
  5.5 0.2 fusion.2
  5.7 0.2 fusion.11
  5.8 0.1 fusion.20
  6.0 0.1 select_reduce_fusion.1
  6.1 0.0 copy-start.1
  6.1 4.9 %select_reduce_fusion = s32[4,768]{1,0:T(4,128)S(1)} fusion(s32[4,3072]{1,0:T(4,128)S(1)} %add.82, s32[4,3072]{1,0:T(4,128)S(1)} %get-tuple-element.15), kind=kLoop, calls=%fused_computation | loop fusion | flops 28308480 | bytes 110592 | tf_op jit(solution)/shard_map/reduce_sum | solution.py:52
  11.0 1.5 copy.18
  12.5 1.0 multiply_bitcast_fusion.second_turned
  13.5 2.3 copy.17
  15.8 1.7 copy.25
  17.4 1.7 copy.21.landing
  19.1 294.0 %shard_map.85 = (bf16[8,128,3072]{2,1,0:T(8,128)(2,1)}, bf16[8,128,3072]{2,1,0:T(8,128)(2,1)}, bf16[8,128,3072]{2,1,0:T(8,128)(2,1)}, bf16[4,8,128,768]{3,2,1,0:...) custom-call(bf16[8,128,3072]{2,1,0:T(8,128)(2,1)} %bitcast.37, ...), custom_call_target="tpu_custom_call" | custom-call | tf_op jit(solution)/shard_map/pallas_call | solution.py:408
  313.1 0.0 copy-done.1
  313.1 0.0 copy-start
  313.2 36.7 %shard_map.86 = (f32[24,128,128]{2,1,0:T(8,128)}, f32[24,128,128]{2,1,0:T(8,128)}) custom-call(bf16[4,1024,768]{2,1,0:T(8,128)(2,1)} %bitcast.43, s32[1,3072]{1,0:T(1,128)} %bitcast.47, f32[1,1]{1,0:T(1,128)S(6)} %convert_element_type.38.kept, bf16[1024,3072]{1,0:T(8,128)(2,1)} %bitcast.42, bf16[1024,3072]{1,0:T(8,128)(2,1)} %bitcast.38, ...), custom_call_target="tpu_custom_call" | custom-call | tf_op jit(solution)/shard_map/pallas_call | solution.py:443
  349.9 0.0 copy-done
  349.9 2.7 copy.29
  (9 shorter events, 0.1 us)
Async XLA Ops:
  6.1 307.1 %copy-start.1 = (s32[24,128]{1,0:T(8,128)}, s32[24,128]{1,0:T(8,128)S(1)}, u32[]{:S(2)}) copy-start(s32[24,128]{1,0:T(8,128)S(1)} %select_reduce_fusion.1) | copy-start | bytes 36868
  313.1 36.7 %copy-start = (bf16[8,128,3072]{2,1,0:T(8,128)(2,1)S(1)}, bf16[8,128,3072]{2,1,0:T(8,128)(2,1)}, u32[]{:S(2)}) copy-start(bf16[8,128,3072]{2,1,0:T(8,128)(2,1)} %get-tuple-element.9) | copy-start | bytes 18874372

commit v4 on v3

--- a/solution.py
+++ b/solution.py
@@ -78,6 +78,10 @@
     chunks, rows, feats = inputs.shape
     size = first.shape[1]
     depth = arrived.shape[0]
+
+    def columns(origin):
+        return pl.ds(pl.multiple_of(origin * slots, LANES), slots)
+
     tile = 512 if feats % 512 == 0 else 256
     parts = 3 if feats // tile % 3 == 0 else 1
     part = feats // parts
@@ -195,14 +199,16 @@
     def swap(offset):
         return pltpu.make_async_remote_copy(
             src_ref=sent_out.at[peer(offset)],
-            dst_ref=came_out.at[group],
+            dst_ref=came_out.at[:, :, columns(group)],
             send_sem=swap_send.at[offset],
             recv_sem=swap_recv.at[offset],
             device_id={"tensor": peer(offset)},
             device_id_type=MESH,
         )
 
-    own_swap = pltpu.make_async_copy(sent_out.at[group], came_out.at[group], swap_own)
+    own_swap = pltpu.make_async_copy(
+        sent_out.at[group], came_out.at[:, :, columns(group)], swap_own
+    )
 
     def start_swap():
         for offset in range(1, groups):
@@ -217,7 +223,7 @@
         target = peer(offset)
         return pltpu.make_async_remote_copy(
             src_ref=sending.at[slot, target],
-            dst_ref=arrived.at[lax.rem(chunk, depth), group],
+            dst_ref=arrived.at[lax.rem(chunk, depth), :, columns(group)],
             send_sem=send_sem.at[slot, offset],
             recv_sem=recv_sem.at[chunk, offset],
             device_id={"tensor": target},
@@ -228,7 +234,7 @@
         origin = source(offset)
         pltpu.make_async_remote_copy(
             src_ref=sending.at[slot, origin],
-            dst_ref=arrived.at[lax.rem(chunk, depth), origin],
+            dst_ref=arrived.at[lax.rem(chunk, depth), :, columns(origin)],
             send_sem=send_sem.at[slot, offset],
             recv_sem=recv_sem.at[chunk, offset],
             device_id={"tensor": origin},
@@ -276,9 +282,9 @@
             target = peer(offset)
             sending[slot, target] = dot(cotangents[chunk], back_mix[target]).astype(jnp.bfloat16)
             mix_copy(chunk, slot, offset).start()
-        arrived[lax.rem(chunk, depth), group] = dot(cotangents[chunk], back_mix[group]).astype(
-            jnp.bfloat16
-        )
+        arrived[lax.rem(chunk, depth), :, columns(group)] = dot(
+            cotangents[chunk], back_mix[group]
+        ).astype(jnp.bfloat16)
 
     def leave(chunk, slot):
         store_grad(chunk, slot).wait()
@@ -303,11 +309,7 @@
         def one_tile(index, _):
             start = pl.multiple_of(index * tile, tile)
             at = pl.ds(start, tile)
-            total = dot(arrived[held, 0], leaving[0:slots, at])
-            for origin in range(1, groups):
-                total += dot(
-                    arrived[held, origin], leaving[origin * slots : (origin + 1) * slots, at]
-                )
+            total = dot(arrived[held], leaving[:, at])
             before = (total * slopes[slot, :, at].astype(jnp.float32)).astype(jnp.bfloat16)
             befores[slot, :, at] = before
             for piece in range(tile // size):
@@ -366,19 +368,17 @@
 
 
 def weight_kernel(came, landing, kept, cotangents, inputs, befores, first_out, second_out):
-    groups, tokens, slots = came.shape
     count, size, _ = first_out.shape
     where = landing[...]
-    mixed = jnp.zeros((tokens, where.shape[1]), jnp.float32)
-    for origin in range(groups):
-        slot = lax.broadcasted_iota(jnp.int32, (slots, where.shape[1]), 0) + origin * slots
-        spread = jnp.where(slot == where, 1.0, 0.0).astype(jnp.bfloat16)
-        mixed += dot(came[origin], spread)
-    mixed = mixed.astype(jnp.bfloat16)
+    slot = lax.broadcasted_iota(jnp.int32, (came.shape[1], where.shape[1]), 0)
+    spread = jnp.where(slot == where, 1.0, 0.0).astype(jnp.bfloat16)
+    mixed = dot(came[...], spread).astype(jnp.bfloat16)
+    second = dot(mixed, cotangents[...], 0, 0) * kept[0, 0]
+    first = dot(inputs[...], befores[...], 0, 0)
     for piece in range(count):
         at = slice(piece * size, (piece + 1) * size)
-        second_out[piece] = dot(mixed[:, at], cotangents[:, at], 0, 0) * kept[0, 0]
-        first_out[piece] = dot(inputs[:, at], befores[:, at], 0, 0)
+        second_out[piece] = second[at, at]
+        first_out[piece] = first[at, at]
 
 
 def on_device(section_inputs, out_grad, w_first, w_second, drop_flags, perm):
@@ -407,14 +407,15 @@
     swapped = (groups, chunks, rows, slots)
     grads, befores, cotangents, came, _, _ = pl.pallas_call(
         functools.partial(relay_kernel, sections, groups, slots),
-        out_shape=[made(*chunked)] * 3 + [made(*swapped)] * 2 + [made(*chunked)],
+        out_shape=[made(*chunked)] * 3
+        + [made(chunks, rows, groups * slots), made(*swapped), made(*chunked)],
         in_specs=[anywhere] * 2 + [vmem] * 5,
         out_specs=[anywhere] * 6,
         scratch_shapes=[
             room(groups * slots, feats),
             room(groups, feats, slots),
             room(*chunked),
-            room(depth, groups, rows, slots),
+            room(depth, rows, groups * slots),
             room(2, rows, feats),
             room(2, rows, feats),
             room(2, rows, feats),
@@ -445,7 +446,7 @@
         grid=(feats // wide,),
         out_shape=[weights] * 2,
         in_specs=[
-            pl.BlockSpec((groups, tokens, slots), lambda i: (0, 0, 0)),
+            pl.BlockSpec((tokens, groups * slots), lambda i: (0, 0)),
             pl.BlockSpec((1, wide), lambda i: (0, i)),
             pl.BlockSpec(memory_space=pltpu.SMEM),
             tall, tall, tall,
@@ -453,7 +454,7 @@
         out_specs=[out] * 2,
         compiler_params=pltpu.CompilerParams(vmem_limit_bytes=56 * 2**20),
     )(
-        came.reshape(groups, tokens, slots),
+        came.reshape(tokens, groups * slots),
         landing[None, :],
         kept.astype(jnp.float32).reshape(1, 1),
         cotangents.reshape(tokens, feats),

time: 353 us -> 351 us (level)
  no operation moved by 1% of the time
where the time goes in v4:
time: 351 us
  Pallas kernels  329 us (94%)
  local copies, waits for them, and re-layouts  10.8 us (3%)
  other arithmetic  9 us (3%)
    pallas_call x1, Pallas kernels, on_device(): pl.pallas_call(functools.partial(relay_kernel, sections, groups, slots),...  294 us
    pallas_call x1, Pallas kernels, on_device(): pl.pallas_call(weight_kernel, grid=(feats // wide,), out_shape=[weights]...  35.3 us
    unnamed x9, local copies, waits for them, and re-layouts  8.18 us

profile of v4, /device:TPU:0, one launch (start us, length us, event | category | flops | bytes accessed | tf_op | source)
XLA Modules:
  0.0 351.0 jit_solution(890455334891213986)
XLA Ops:
  1.3 1.1 and_reduce_fusion
  2.5 0.5 broadcast.166
  3.0 1.8 fusion.37
  4.8 0.2 fusion.3
  5.0 0.2 fusion.10
  5.2 0.1 fusion.22
  5.3 0.1 add_bitcast_fusion
  5.5 0.2 fusion.2
  5.7 0.2 fusion.11
  5.8 0.1 fusion.20
  6.0 0.1 select_reduce_fusion.1
  6.1 0.0 copy-start.1
  6.1 4.9 %select_reduce_fusion = s32[4,768]{1,0:T(4,128)S(1)} fusion(s32[4,3072]{1,0:T(4,128)S(1)} %add.82, s32[4,3072]{1,0:T(4,128)S(1)} %get-tuple-element.15), kind=kLoop, calls=%fused_computation | loop fusion | flops 28308480 | bytes 110592 | tf_op jit(solution)/shard_map/reduce_sum | solution.py:52
  11.0 1.5 copy.18
  12.5 1.0 multiply_bitcast_fusion.second_turned
  13.5 2.3 copy.17
  15.8 1.7 copy.25
  17.4 1.7 copy.21.landing
  19.1 293.8 %shard_map.85 = (bf16[8,128,3072]{2,1,0:T(8,128)(2,1)}, bf16[8,128,3072]{2,1,0:T(8,128)(2,1)}, bf16[8,128,3072]{2,1,0:T(8,128)(2,1)}, bf16[8,128,3072]{2,1,0:T(8...) custom-call(bf16[8,128,3072]{2,1,0:T(8,128)(2,1)} %bitcast.37, ...), custom_call_target="tpu_custom_call" | custom-call | tf_op jit(solution)/shard_map/pallas_call | solution.py:408
  312.9 0.0 copy-done.1
  312.9 0.0 copy-start
  312.9 35.3 %shard_map.86 = (f32[24,128,128]{2,1,0:T(8,128)}, f32[24,128,128]{2,1,0:T(8,128)}) custom-call(bf16[1024,3072]{1,0:T(8,128)(2,1)} %bitcast.43, s32[1,3072]{1,0:T(1,128)} %bitcast.47, f32[1,1]{1,0:T(1,128)S(6)} %convert_element_type.38.kept, bf16[1024,3072]{1,0:T(8,128)(2,1)} %bitcast.42, bf16[1024,3072]{1,0:T(8,128)(2,1)} %bitcast.38, ...), custom_call_target="tpu_custom_call" | custom-call | tf_op jit(solution)/shard_map/pallas_call | solution.py:444
  348.2 0.0 copy-done
  348.2 2.7 copy.29
  (9 shorter events, 0.1 us)
Async XLA Ops:
  6.1 306.9 %copy-start.1 = (s32[24,128]{1,0:T(8,128)}, s32[24,128]{1,0:T(8,128)S(1)}, u32[]{:S(2)}) copy-start(s32[24,128]{1,0:T(8,128)S(1)} %select_reduce_fusion.1) | copy-start | bytes 36868
  312.9 35.3 %copy-start = (bf16[8,128,3072]{2,1,0:T(8,128)(2,1)S(1)}, bf16[8,128,3072]{2,1,0:T(8,128)(2,1)}, u32[]{:S(2)}) copy-start(bf16[8,128,3072]{2,1,0:T(8,128)(2,1)} %get-tuple-element.9) | copy-start | bytes 18874372
